TPU v7x, 512 devices: a whole 4x8x8 slice. The times are simulated.
512 devices in a mesh: grp: 16 (over y, x_hi), dev: 32 (over z, x_lo, core).
Axes of the slice: x: 4 (x_hi: 2, x_lo: 2; x = x_hi * 2 + x_lo), y: 8, z: 8, core: 2. Of those that a mesh axis runs over, the one named last changes fastest.
Arguments:
- velocities: bfloat16 [8192, 240, 512], P(('grp', 'dev')), may hold values from -6 to 6
- mass_root: float32 [240], replicated, may hold values from 1 to 4
- eigvec: float32 [2, 8, 240, 240], replicated, may hold values from -0.375 to 0.375
- q_points: int32 [3, 8], replicated, may hold values from 0 to 7
- cell_offsets: int32 [3, 512], replicated, may hold values from 0 to 7, as said below
Outputs:
- spectrum: float32 [16, 1920, 512], P('grp', 'dev')
Inputs may be any that keep to these rules, and one draw needn't show every extreme that they name: `cell_offsets`: each cell of the 8 x 8 x 8 lattice appears exactly once.
All inputs are finite; a program needn't handle non-finite values.
Results may differ from a plain program's by a relative error of at most 0.0003.
Values sent between devices are 32-bit elements; how exact they have to be, the bound alone decides.
No kernel may reach another device: no remote copies, remote signals or barrier semaphores. Data moves between devices by JAX's collectives and lax.ppermute only.
A program may use at most 64 MiB of HBM per device.

v0:
```python
import math

import jax
import jax.numpy as jnp
from jax import lax
from jax.sharding import PartitionSpec as P

LAT = 8
CELLS = 512


def phase_table(q_points, cell_offsets, lattice, cells):
    products = jnp.sum(cell_offsets[:, :, None] * q_points[:, None, :], axis=0) % lattice
    angles = products.astype(jnp.float32) * (2.0 * math.pi / lattice)
    both = jnp.concatenate([jnp.cos(angles), jnp.sin(angles)], axis=1) * cells ** (-0.5)
    return both.astype(jnp.bfloat16)


def project_frames(frames_in, phases, mass_root, eigvec):
    nframes, ndof, ncells = frames_in.shape
    nqpts = phases.shape[1] // 2
    summed = jnp.dot(
        frames_in.reshape(nframes * ndof, ncells), phases, preferred_element_type=jnp.float32
    )
    summed = summed.reshape(nframes, ndof, 2, nqpts) * mass_root[None, :, None, None]
    real_s = summed[:, :, 0, :]
    imag_s = summed[:, :, 1, :]
    highest = lax.Precision.HIGHEST
    real_u = jnp.einsum("kbd,fdk->kbf", eigvec[0], real_s, precision=highest) + jnp.einsum(
        "kbd,fdk->kbf", eigvec[1], imag_s, precision=highest
    )
    imag_u = jnp.einsum("kbd,fdk->kbf", eigvec[0], imag_s, precision=highest) - jnp.einsum(
        "kbd,fdk->kbf", eigvec[1], real_s, precision=highest
    )
    return jnp.stack([real_u, imag_u]).reshape(2, nqpts * ndof, nframes)


def rotate(real_x, imag_x, angles):
    cosine = jnp.cos(angles)
    sine = jnp.sin(angles)
    return (real_x * cosine + imag_x * sine, imag_x * cosine - real_x * sine)


def dft_last(real_x, imag_x):
    length = real_x.shape[-1]
    offsets = lax.iota(jnp.int32, length)
    angles = (offsets[:, None] * offsets[None, :] % length).astype(jnp.float32) * (
        2.0 * math.pi / length
    )
    cosine = jnp.cos(angles)
    sine = jnp.sin(angles)
    flat_real = real_x.reshape(-1, length)
    flat_imag = imag_x.reshape(-1, length)
    highest = lax.Precision.HIGHEST
    real_out = jnp.dot(flat_real, cosine, precision=highest) + jnp.dot(
        flat_imag, sine, precision=highest
    )
    imag_out = jnp.dot(flat_imag, cosine, precision=highest) - jnp.dot(
        flat_real, sine, precision=highest
    )
    return (real_out.reshape(real_x.shape), imag_out.reshape(imag_x.shape))


def per_device(velocities, mass_root, eigvec, q_points, cell_offsets):
    phases = phase_table(q_points, cell_offsets, LAT, CELLS)
    series = project_frames(velocities, phases, mass_root, eigvec)
    exchanged = lax.all_to_all(series, "dev", split_axis=1, concat_axis=2, tiled=True)
    length = exchanged.shape[2]
    groups = lax.axis_size("grp")
    total_len = length * groups
    group_idx = lax.axis_index("grp")
    freq_low = lax.iota(jnp.int32, 1 * lax.axis_size("grp"))
    times = group_idx * length + lax.iota(jnp.int32, length)
    angles = (freq_low[:, None] * times[None, :] % total_len).astype(jnp.float32) * (
        2.0 * math.pi / total_len
    )
    real_y, imag_y = rotate(exchanged[0][None], exchanged[1][None], angles[:, None, :])
    real_o, imag_o = dft_last(real_y, imag_y)
    summed = lax.psum_scatter(
        jnp.stack([real_o, imag_o], axis=1), "grp", scatter_dimension=0, tiled=True
    )
    real_f = summed[:, 0]
    imag_f = summed[:, 1]
    return (real_f * real_f + imag_f * imag_f) / total_len


def solution(mesh):
    return jax.shard_map(
        per_device,
        mesh=mesh,
        in_specs=(P(("grp", "dev"), None, None), P(), P(), P(), P()),
        out_specs=P("grp", "dev", None),
        check_vma=False,
    )
```

profile of v0, /device:TPU:1, one launch (start us, length us, event | category | flops | bytes accessed | tf_op | source)
XLA Modules:
  0.0 319.7 jit_solution(890773390316866770)
XLA Ops:
  6.5 0.8 multiply_reduce_fusion
  7.4 3.2 %convolution_bitcast_fusion = f32[3840,16]{0,1:T(8,128)S(1)} fusion(bf16[3840,512]{1,0:T(8,128)(2,1)} %bitcast.55, f32[512,8]{0,1:T(8,128)S(1)} %get-tuple-element.10, f32[512,8]{0,1:T(8,128)S(1)} %get-tuple-element.9), kind=kOutput, calls=%fused_computation | convolution fusion | flops 62939136 | bytes 4210688 | tf_op jit(solution)/shard_map/dot_general | solution.py:22
  10.7 0.3 reshape.125
  11.0 3.4 %fusion.2 = f32[8,16,240]{2,1,0:T(8,128)S(1)} fusion(f32[2,8,240,240]{3,2,1,0:T(8,128)} %param.7, f32[16,240,2,8]{1,0,3,2:T(8,128)S(1)} %broadcast_multiply_fusion), kind=kOutput, calls=%fused_computation.6 | convolution fusion | flops 88473600 | bytes 2220032 | tf_op jit(solution)/shard_map/kbd,fdk->kbf/dot_general | solution.py:29
  14.4 3.3 %fusion = f32[8,16,240]{2,1,0:T(8,128)S(1)} fusion(f32[2,8,240,240]{3,2,1,0:T(8,128)} %param.7, f32[16,240,2,8]{1,0,3,2:T(8,128)S(1)} %broadcast_multiply_fusion), kind=kOutput, calls=%fused_computation.4 | convolution fusion | flops 88473600 | bytes 2220032 | tf_op jit(solution)/shard_map/kbd,fdk->kbf/dot_general | solution.py:32
  17.7 1.7 fusion.15
  19.6 3.3 %fusion.21 = f32[8,240,16]{1,2,0:T(8,128)S(1)} fusion(f32[8,16,240]{2,1,0:T(8,128)S(1)} %fusion, f32[2,8,240,240]{3,2,1,0:T(8,128)} %param.7, f32[16,240,2,8]{1,0,3,2:T(8,128)S(1)} %broadcast_multiply_fusion), kind=kOutput, calls=%fused_computation.24 | convolution fusion | flops 88504320 | bytes 2351104 | tf_op jit(solution)/shard_map/kbd,fdk->kbf/dot_general | solution.py:32
  23.1 0.9 copy.26
  24.0 3.3 %reshape.127 = f32[32,1,1920]{2,1,0:T(1,128)} reshape(f32[1920,2,16]{2,1,0:T(2,128)S(1)} %bitcast.53) | data formatting | bytes 491520
  27.3 12.9 %all-to-all-start = ((f32[32,1,1920]{2,1,0:T(1,128)}), f32[32,1,1920]{2,1,0:T(1,128)S(1)}, u32[]{:S(2)}, u32[]{:S(2)}) async-start(f32[32,1,1920]{2,1,0:T(1,128)} %reshape.127), calls=%async_computation | async-start | bytes 491520 | tf_op jit(solution)/shard_map/all_to_all | solution.py:67
  40.2 0.2 all-reduce.3.cloned.1.call-start
  40.6 10.8 %all-to-all-done = f32[32,1,1920]{2,1,0:T(1,128)S(1)} async-done(((f32[32,1,1920]{2,1,0:T(1,128)}), f32[32,1,1920]{2,1,0:T(1,128)S(1)}, u32[]{:S(2)}, u32[]{:S(2)}) %all-to-all-start) | async-done | bytes 245792 | tf_op jit(solution)/shard_map/all_to_all | solution.py:67
  51.4 0.5 broadcast.125
  51.9 1.2 reduce
  53.2 2.5 reshape.128
  55.7 1.1 copy.33
  56.8 0.2 copy.28
  57.1 0.2 copy.30
  57.4 1.9 multiply_add_fusion
  59.3 2.7 add.78
  62.0 9.8 %fusion.34 = f32[960,512]{1,0:T(8,128)} fusion(f32[960,512]{1,0:T(8,128)} %add.78), kind=kOutput, calls=%fused_computation.34 | convolution fusion | flops 3023568896 | bytes 3932160 | tf_op jit(solution)/shard_map/dot_general | solution.py:55
  71.9 1.5 sub.19
  73.4 10.0 %fusion.32 = f32[960,512]{1,0:T(8,128)} fusion(f32[960,512]{1,0:T(8,128)} %sub.19), kind=kOutput, calls=%fused_computation.33 | convolution fusion | flops 3023568896 | bytes 3932160 | tf_op jit(solution)/shard_map/dot_general | solution.py:58
  83.3 8.3 %convolution_add_fusion = f32[960,512]{1,0:T(8,128)} fusion(f32[960,512]{1,0:T(8,128)S(1)} %copy-done.3, f32[960,512]{1,0:T(8,128)S(1)} %copy-done.1), kind=kOutput, calls=%fused_computation.17 | convolution fusion | flops 3024060416 | bytes 5898240 | tf_op jit(solution)/shard_map/dot_general | solution.py:55
  91.7 1.6 stack_reshape.6
  93.3 10.2 %convolution_subtract_fusion = f32[960,512]{1,0:T(8,128)} fusion(f32[960,512]{1,0:T(8,128)} %fusion.32, f32[960,512]{1,0:T(8,128)} %add.78), kind=kOutput, calls=%fused_computation.16 | convolution fusion | flops 3024060416 | bytes 5898240 | tf_op jit(solution)/shard_map/dot_general | solution.py:58
  103.4 2.8 stack_reshape.7
  106.2 2.1 pad_maximum_fusion
  108.3 4.9 %copy.32 = f32[16,2,60,512]{3,1,2,0:T(2,128)} copy(f32[16,2,60,512]{3,2,0,1:T(8,128)S(1)} %pad_maximum_fusion) | data formatting | bytes 7864320 | tf_op jit(solution)/shard_map/stack | solution.py:80
  113.3 1.3 dynamic-slice
  114.6 195.7 %all-reduce.3.cloned.1.call-done = f32[16,2,60,512]{3,1,2,0:T(2,128)} async-done(((f32[16,2,60,512]{3,1,2,0:T(2,128)}), f32[16,2,60,512]{3,1,2,0:T(2,128)}) %all-reduce.3.cloned.1.call-update) | async-done | bytes 3932176
  310.3 2.5 multiply_bitcast_fusion
  (21 shorter events, 1.0 us)
Async XLA Ops:
  7.4 3.5 %copy-start.2 = (f32[240]{0:T(256)S(1)}, f32[240]{0:T(256)}, u32[]{:S(2)}) copy-start(f32[240]{0:T(256)} %param.6) | copy-start | bytes 2884
  11.0 6.7 %copy-start = (f32[2,8,240,240]{3,2,1,0:T(8,128)S(1)}, f32[2,8,240,240]{3,2,1,0:T(8,128)}, u32[]{:S(2)}) copy-start(f32[2,8,240,240]{3,2,1,0:T(8,128)} %param.7) | copy-start | bytes 11059204
  27.3 24.1 %all-to-all-start = ((f32[32,1,1920]{2,1,0:T(1,128)}), f32[32,1,1920]{2,1,0:T(1,128)S(1)}, u32[]{:S(2)}, u32[]{:S(2)}) async-start(f32[32,1,1920]{2,1,0:T(1,128)} %reshape.127), calls=%async_computation | async-start | bytes 491520 | tf_op jit(solution)/shard_map/all_to_all | solution.py:67
  40.2 270.0 %all-reduce.3.cloned.1.call-start = ((), (), s32[]{:S(2)}) async-start(), calls=%async_computation.1 | async-start | bytes 7864320
  73.4 10.0 %copy-start.1 = (f32[960,512]{1,0:T(8,128)S(1)}, f32[960,512]{1,0:T(8,128)}, u32[]{:S(2)}) copy-start(f32[960,512]{1,0:T(8,128)} %sub.19) | copy-start | bytes 5898244
  73.4 10.0 %copy-start.3 = (f32[960,512]{1,0:T(8,128)S(1)}, f32[960,512]{1,0:T(8,128)}, u32[]{:S(2)}) copy-start(f32[960,512]{1,0:T(8,128)} %fusion.34) | copy-start | bytes 5898244
Sparse Core Ops, SparseCore 0:
  113.4 196.8 all-reduce.2
where the time goes:
time: 323 us; the launch traced here: 320 us
  waiting for transfers between devices  207 us (64%)
  matrix products  53.2 us (16%)
  local copies, waits for them, and re-layouts  24.4 us (8%)
  between operations  13.6 us (4%)
  starting transfers between devices  13.1 us (4%)
  other arithmetic  8.82 us (3%)
    unnamed x2, waiting for transfers between devices  196 us
    all_to_all x1, starting transfers between devices, per_device(): lax.all_to_all(series, 'dev', split_axis=1, concat_axis=2, tiled=True)  12.9 us
    all_to_all x1, waiting for transfers between devices, per_device(): lax.all_to_all(series, 'dev', split_axis=1, concat_axis=2, tiled=True)  10.8 us
    dot_general x1, matrix products, dft_last(): jnp.dot(flat_real, sine, precision=highest)  10.2 us
    dot_general x1, matrix products, dft_last(): jnp.dot(flat_imag, cosine, precision=highest)  9.97 us
    dot_general x1, matrix products, dft_last(): jnp.dot(flat_real, cosine, precision=highest)  9.84 us
    another operation x3, local copies, waits for them, and re-layouts, per_device(): jnp.stack([real_o, imag_o], axis=1)  9.3 us
    dot_general x1, matrix products, dft_last(): jnp.dot(flat_imag, sine, precision=highest)  8.35 us
  transfers between devices with their start and end apart: 2, of which 2 were waited for; matrix products, arithmetic and copies ran while one was open for 0% of the time, Pallas kernels for 0%

commit v1 on v0

v1 whole, which is shorter than its diff:
```python
import functools
import math

import jax
import jax.numpy as jnp
import numpy as np
from jax import lax
from jax.experimental import pallas as pl
from jax.experimental.pallas import tpu as pltpu
from jax.sharding import PartitionSpec as P

LAT = 8
CELLS = 512
DOF = 240
QPTS = 8
TOTAL = 8192
N_GRP = 16
N_DEV = 32
FRAMES = 16
PER_DEV = 60
QUAD = 4
SPAN = 512
F32 = jnp.float32
BF16 = jnp.bfloat16


def split(x):
    hi = x.astype(BF16)
    return hi, (x - hi.astype(F32)).astype(BF16)


def dot_t(a, b):
    return lax.dot_general(a, b, (((1,), (1,)), ((), ())), preferred_element_type=F32)


def dot(a, b):
    return jnp.dot(a, b, preferred_element_type=F32)


def cosine_of(eighths):
    one = CELLS**-0.5
    half = math.sqrt(0.5) * CELLS**-0.5
    near = jnp.where((eighths == 1) | (eighths == 7), half, 0.0)
    far = jnp.where((eighths == 3) | (eighths == 5), -half, near)
    return jnp.where(eighths == 0, one, jnp.where(eighths == 4, -one, far))


def project_kernel(
    q_ref, cell_ref, mass_ref, vel_hbm, eig_hbm, out_ref, vel, eig, summed, series, vel_sem, eig_sem
):
    vel_copies = []
    for part in range(4):
        frames = pl.ds(part * 4, 4)
        copy = pltpu.make_async_copy(vel_hbm.at[frames], vel.at[frames], vel_sem.at[part])
        copy.start()
        vel_copies.append(copy)
    eig_copies = []
    for half in range(2):
        ks = pl.ds(half * 4, 4)
        for ri in range(2):
            copy = pltpu.make_async_copy(eig_hbm.at[ri, ks], eig.at[ri, ks], eig_sem.at[half * 2 + ri])
            copy.start()
            eig_copies.append(copy)

    row = lax.broadcasted_iota(jnp.int32, (QPTS, CELLS), 0)
    products = jnp.zeros((QPTS, CELLS), jnp.int32)
    for j in range(3):
        column = jnp.zeros((QPTS, CELLS), jnp.int32)
        for k in range(QPTS):
            column = jnp.where(row == k, q_ref[j, k], column)
        products = products + column * cell_ref[j : j + 1, :]
    eighths = products & (LAT - 1)
    phases = jnp.concatenate(
        [cosine_of(eighths), cosine_of((eighths + 6) & (LAT - 1))], axis=0
    ).astype(BF16)

    mass = mass_ref[...]
    for part in range(4):
        vel_copies[part].wait()
        for t in range(part * 4, part * 4 + 4):
            sums = dot_t(phases, vel[t]) * mass
            summed[0, t * 16 : (t + 1) * 16, :] = sums[:, :128]
            summed[1, t * 16 : (t + 1) * 16, : DOF - 128] = sums[:, 128:]

    series[1920:1928, :] = jnp.zeros((8, 128), F32)
    for half in range(2):
        first, second = [], []
        for kk in range(4):
            k = half * 4 + kk
            real, imag = [
                jnp.concatenate(
                    [summed[lanes, pl.ds(start, 16, stride=16), :] for lanes in range(2)], axis=1
                )[:, :DOF]
                for start in (k, 8 + k)
            ]
            first += [real, imag]
            second += [imag, -real]
        first = jnp.concatenate(split(jnp.concatenate(first, axis=0)), axis=0)
        second = jnp.concatenate(split(jnp.concatenate(second, axis=0)), axis=0)
        eig_copies[half * 2].wait()
        eig_copies[half * 2 + 1].wait()
        for kk in range(4):
            k = half * 4 + kk
            real_hi, real_lo = split(eig[0, k])
            imag_hi, imag_lo = split(eig[1, k])
            both = dot_t(real_hi, first) + dot_t(real_lo, first)
            both = both + dot_t(imag_hi, second) + dot_t(imag_lo, second)
            series[k * DOF : (k + 1) * DOF, :] = both[:, :128] + both[:, 128:]

    lane_quad = lax.broadcasted_iota(jnp.int32, (16, 128), 1) // 32
    for chunk in range(N_DEV):
        kk = chunk // 4 % 4
        message = None
        for i in range(QUAD):
            part = series[pl.ds(chunk * PER_DEV + i, 16, stride=QUAD), :]
            turn = (i - kk) * 32 % 128
            if turn:
                part = pltpu.roll(part, turn, 1)
            message = part if message is None else jnp.where(lane_quad == i, part, message)
        out_ref[chunk * 16 : (chunk + 1) * 16, :] = message


def project(velocities, mass_root, eigvec, q_points, cell_offsets):
    return pl.pallas_call(
        project_kernel,
        out_shape=jax.ShapeDtypeStruct((512, 128), F32),
        in_specs=[
            pl.BlockSpec(memory_space=pltpu.SMEM),
            pl.BlockSpec(memory_space=pltpu.VMEM),
            pl.BlockSpec(memory_space=pltpu.VMEM),
            pl.BlockSpec(memory_space=pl.ANY),
            pl.BlockSpec(memory_space=pl.ANY),
        ],
        out_specs=pl.BlockSpec(memory_space=pltpu.VMEM),
        scratch_shapes=[
            pltpu.VMEM((FRAMES, DOF, CELLS), BF16),
            pltpu.VMEM((2, QPTS, DOF, DOF), F32),
            pltpu.VMEM((2, 256, 128), F32),
            pltpu.VMEM((1928, 128), F32),
            pltpu.SemaphoreType.DMA((4,)),
            pltpu.SemaphoreType.DMA((4,)),
        ],
        compiler_params=pltpu.CompilerParams(vmem_limit_bytes=32 * 1024 * 1024),
        name="project",
    )(q_points, cell_offsets, mass_root.reshape(1, DOF), velocities, eigvec)


def transform_kernel(x_ref, low_ref, cos_ref, sin_ref, dft_ref, out_ref):
    lane = lax.broadcasted_iota(jnp.int32, (16, 128), 1)
    tiles = []
    for j in range(4):
        blocks = [x_ref[(8 * j + d) * 16 : (8 * j + d + 1) * 16, :] for d in range(8)]
        for bit in (4, 2, 1):
            width = bit * 16
            keep = (lane & width) == 0
            for a in range(8):
                if a & bit:
                    continue
                b = a | bit
                u, v = blocks[a], blocks[b]
                blocks[a] = jnp.where(keep, u, pltpu.roll(v, width, 1))
                blocks[b] = jnp.where(keep, pltpu.roll(u, 128 - width, 1), v)
        tiles.append(jnp.concatenate(blocks, axis=0))
    gathered = jnp.concatenate(tiles, axis=1)
    stacked = jnp.concatenate(split(gathered), axis=0)
    low = dot(low_ref[0], stacked) + dot(low_ref[1], stacked)
    real, imag = low[:64], low[64:]
    cosine, sine = cos_ref[...], sin_ref[...]
    turned = jnp.concatenate(
        [real * cosine + imag * sine, imag * cosine - real * sine], axis=0
    )
    hi, lo = split(turned)
    by_cos = dot(hi, dft_ref[0]) + dot(lo, dft_ref[0]) + dot(hi, dft_ref[2])
    by_sin = dot(hi, dft_ref[1]) + dot(lo, dft_ref[1]) + dot(hi, dft_ref[3])
    real = by_cos[:64] + by_sin[64:]
    imag = by_cos[64:] - by_sin[:64]
    power = (real * real + imag * imag) * (1.0 / TOTAL)
    for j in range(4):
        for i in range(QUAD):
            out_ref[pl.ds(j * 4 + i, 16, stride=16), :] = power[
                i * 16 : (i + 1) * 16, j * 128 : (j + 1) * 128
            ]


def split_np(x):
    hi = x.astype(np.float32).astype(jnp.bfloat16)
    lo = (x - hi.astype(np.float64)).astype(np.float32).astype(jnp.bfloat16)
    return hi, lo


@functools.cache
def tables():
    g = np.arange(16)
    theta = 2.0 * np.pi * (g[:, None] * g[None, :] % 16) / 16
    low = np.zeros((2, QUAD, 16, QUAD, 2, 16))
    for i in range(QUAD):
        low[0, i, :, i, 0] = np.cos(theta)
        low[0, i, :, i, 1] = np.sin(theta)
        low[1, i, :, i, 0] = -np.sin(theta)
        low[1, i, :, i, 1] = np.cos(theta)
    hi, lo = split_np(low.reshape(128, 128))
    low = np.stack([np.concatenate([hi, hi], axis=1), np.concatenate([lo, lo], axis=1)])
    s = np.arange(SPAN)
    twist = 2.0 * np.pi * np.tile(g[:, None] * s[None, :], (QUAD, 1)) / TOTAL
    full = 2.0 * np.pi * (s[:, None] * s[None, :] % SPAN) / SPAN
    cos_hi, cos_lo = split_np(np.cos(full))
    sin_hi, sin_lo = split_np(np.sin(full))
    dft = np.stack([cos_hi, sin_hi, cos_lo, sin_lo])
    return low, np.cos(twist).astype(np.float32), np.sin(twist).astype(np.float32), dft


def transform(x):
    return pl.pallas_call(
        transform_kernel,
        out_shape=jax.ShapeDtypeStruct((256, 128), F32),
        in_specs=[pl.BlockSpec(memory_space=pltpu.VMEM)] * 5,
        out_specs=pl.BlockSpec(memory_space=pltpu.VMEM),
        compiler_params=pltpu.CompilerParams(vmem_limit_bytes=32 * 1024 * 1024),
        name="transform",
    )(x, *[jnp.asarray(table) for table in tables()])


def order_kernel(x_ref, out_ref, rows):
    for j in range(4):
        for i in range(QUAD):
            rows[pl.ds(i, 16, stride=QUAD), :] = x_ref[pl.ds(j * 4 + i, 16, stride=16), :]
        out_ref[:, j * 128 : (j + 1) * 128] = rows[:PER_DEV, :]


def order(x):
    return pl.pallas_call(
        order_kernel,
        out_shape=jax.ShapeDtypeStruct((PER_DEV, SPAN), F32),
        in_specs=[pl.BlockSpec(memory_space=pltpu.VMEM)],
        out_specs=pl.BlockSpec(memory_space=pltpu.VMEM),
        scratch_shapes=[pltpu.VMEM((64, 128), F32)],
        name="order",
    )(x)


def per_device(velocities, mass_root, eigvec, q_points, cell_offsets):
    messages = project(velocities, mass_root, eigvec, q_points, cell_offsets)
    frames = lax.all_to_all(
        messages.reshape(512, 1, 128), ("dev", "grp"), 0, 0, tiled=True
    )
    power = transform(frames.reshape(512, 128))
    spectra = lax.all_to_all(power.reshape(16, 16, 128), "grp", 0, 0, tiled=True)
    return order(spectra.reshape(256, 128))[None]


def solution(mesh):
    return jax.shard_map(
        per_device,
        mesh=mesh,
        in_specs=(P(("grp", "dev"), None, None), P(), P(), P(), P()),
        out_specs=P("grp", "dev", None),
        check_vma=False,
    )
```

time: 323 us -> 69.8 us (0.22)
  waiting for transfers between devices: 207 us -> 0 us
  matrix products: 53.2 us -> 0 us
  blocking collectives: 0 us -> 52.4 us
  local copies, waits for them, and re-layouts: 24.4 us -> 7.97 us
  between operations: 13.6 us -> 0.04 us
  starting transfers between devices: 13.1 us -> 0 us
  Pallas kernels: 0 us -> 8.99 us
  other arithmetic: 8.82 us -> 0 us
    unnamed x2 -> x0, waiting for transfers between devices: 196 us -> none
    dot_general x9 -> x0, matrix products: 53.2 us -> none  [the longest x1 10.2 us: dft_last(): jnp.dot(flat_real, sine, precision=highest)]
    all_to_all x0 -> x2, blocking collectives: none -> 52.4 us  [the longest x1 39 us: per_device(): lax.all_to_all(messages.reshape(512, 1, 128), ('dev', 'grp'), 0, 0, tiled...]
    all_to_all x1 -> x0, starting transfers between devices: 12.9 us -> none  [per_device(): lax.all_to_all(series, 'dev', split_axis=1, concat_axis=2, tiled=True)]
    all_to_all x1 -> x0, waiting for transfers between devices: 10.8 us -> none  [per_device(): lax.all_to_all(series, 'dev', split_axis=1, concat_axis=2, tiled=True)]
    another operation x6 -> x0, local copies, waits for them, and re-layouts: 10.4 us -> none  [the longest x3 9.3 us: per_device(): jnp.stack([real_o, imag_o], axis=1)]
    pallas_call x0 -> x3, Pallas kernels: none -> 8.99 us  [the longest x1 6.28 us: project(): pl.pallas_call(project_kernel, out_shape=jax.ShapeDtypeStruct((512, 128),...]
    unnamed x11 -> x18, local copies, waits for them, and re-layouts: 7.17 us -> 6.3 us
  transfers between devices with their start and end apart: 2 -> 0, of which waited for: 2 -> 0; matrix products, arithmetic and copies ran while one was open for 0% -> 0% of each run, Pallas kernels for 0% -> 0%
where the time goes in v1:
time: 69.8 us; the launch traced here: 69.4 us
  blocking collectives  52.4 us (75%)
  Pallas kernels  8.99 us (13%)
  local copies, waits for them, and re-layouts  7.97 us (11%)
    all_to_all x1, blocking collectives, per_device(): lax.all_to_all(messages.reshape(512, 1, 128), ('dev', 'grp'), 0, 0, tiled...  39 us
    all_to_all x1, blocking collectives, per_device(): lax.all_to_all(power.reshape(16, 16, 128), 'grp', 0, 0, tiled=True)  13.4 us
    unnamed x18, local copies, waits for them, and re-layouts  6.3 us
    pallas_call x1, Pallas kernels, project(): pl.pallas_call(project_kernel, out_shape=jax.ShapeDtypeStruct((512, 128),...  6.28 us
    broadcast_in_dim x1, local copies, waits for them, and re-layouts, per_device(): return order(spectra.reshape(256, 128))[None]  1.68 us
    pallas_call x1, Pallas kernels, order(): pl.pallas_call(order_kernel, out_shape=jax.ShapeDtypeStruct((PER_DEV, SPA...  1.63 us

profile of v1, /device:TPU:1, one launch (start us, length us, event | category | flops | bytes accessed | tf_op | source)
XLA Modules:
  0.0 69.4 jit_solution(1741261215466912230)
XLA Ops:
  0.0 0.0 copy-start
  0.0 2.1 %copy-done = bf16[16,240,512]{2,1,0:T(8,128)(2,1)S(1)} copy-done((bf16[16,240,512]{2,1,0:T(8,128)(2,1)S(1)}, bf16[16,240,512]{2,1,0:T(8,128)(2,1)}, u32[]{:S(2)}) %copy-start) | copy-done | bytes 3932184
  2.1 0.0 copy-start.1
  2.1 2.1 %copy-done.1 = f32[2,8,240,240]{3,2,1,0:T(8,128)S(1)} copy-done((f32[2,8,240,240]{3,2,1,0:T(8,128)S(1)}, f32[2,8,240,240]{3,2,1,0:T(8,128)}, u32[]{:S(2)}) %copy-start.1) | copy-done | bytes 3686424
  4.2 0.0 copy-start.6
  4.2 0.7 %copy-done.6 = s32[3,512]{1,0:T(4,128)S(1)} copy-done((s32[3,512]{1,0:T(4,128)S(1)}, s32[3,512]{1,0:T(4,128)}, u32[]{:S(2)}) %copy-start.6) | copy-done | bytes 6168
  4.9 0.0 copy-start.7
  4.9 0.7 copy-done.7
  5.6 0.0 copy-start.8
  5.6 0.7 copy-done.8
  6.3 0.0 copy-start.2
  6.3 0.0 copy-start.3
  6.3 0.0 copy-start.4
  6.3 0.0 copy-start.5
  6.3 6.3 %project.1 = f32[512,128]{1,0:T(8,128)S(1)} custom-call(s32[3,8]{1,0:T(4,128)S(1)} %copy-done.7, s32[3,512]{1,0:T(4,128)S(1)} %copy-done.6, f32[1,240]{1,0:T(1,128)S(1)} %bitcast.11, bf16[16,240,512]{2,1,0:T(8,128)(2,1)S(1)} %copy-done, f32[2,8,240,240]{3,2,1,0:T(8,128)S(1)} %copy-done.1), custom_call_target="tpu_custom_call" | custom-call | tf_op jit(solution)/shard_map/project/pallas_call | solution.py:124
  12.6 39.0 %all_to_all.10 = f32[512,1,128]{2,1,0:T(1,128)S(1)} all-to-all(f32[512,1,128]{2,1,0:T(1,128)S(1)} %bitcast.8), channel_id=1, replica_groups=mesh['grp'=16,'dev'=32] {'dev','grp'}, dimensions={0} | all-to-all | bytes 524288 | tf_op jit(solution)/shard_map/all_to_all | solution.py:243
  51.6 0.0 copy-done.2
  51.6 0.0 copy-done.3
  51.6 0.0 copy-done.4
  51.6 0.0 copy-done.5
  51.6 1.1 %transform.1 = f32[256,128]{1,0:T(8,128)S(1)} custom-call(f32[512,128]{1,0:T(8,128)S(1)} %bitcast.9, bf16[2,128,256]{2,1,0:T(8,128)(2,1)S(1)} %copy-done.5, f32[64,512]{1,0:T(8,128)S(1)} %copy-done.4, f32[64,512]{1,0:T(8,128)S(1)} %copy-done.3, bf16[4,512,512]{2,1,0:T(8,128)(2,1)S(1)} %copy-done.2), custom_call_target="tpu_custom_call" | custom-call | tf_op jit(solution)/shard_map/transform/pallas_call | solution.py:213
  52.7 13.4 %all_to_all.11 = f32[16,16,128]{2,1,0:T(8,128)} all-to-all(f32[16,16,128]{2,1,0:T(8,128)S(1)} %bitcast.10), channel_id=1, replica_groups=mesh['grp'=16,'dev'=32] {'grp'}, dimensions={0} | all-to-all | bytes 262144 | tf_op jit(solution)/shard_map/all_to_all | solution.py:247
  66.1 1.6 %order.1 = f32[60,512]{1,0:T(8,128)} custom-call(f32[256,128]{1,0:T(8,128)} %bitcast.12), custom_call_target="tpu_custom_call" | custom-call | tf_op jit(solution)/shard_map/order/pallas_call | solution.py:231
  67.7 1.7 %copy.12 = f32[1,60,512]{2,0,1:T(1,128)} copy(f32[1,60,512]{2,1,0:T(8,128)} %bitcast.13) | data formatting | bytes 245760 | tf_op jit(solution)/shard_map/broadcast_in_dim | solution.py:248
Async XLA Ops:
  0.0 2.1 %copy-start = (bf16[16,240,512]{2,1,0:T(8,128)(2,1)S(1)}, bf16[16,240,512]{2,1,0:T(8,128)(2,1)}, u32[]{:S(2)}) copy-start(bf16[16,240,512]{2,1,0:T(8,128)(2,1)} %vel_hbm.1) | copy-start | bytes 11796484
  2.1 2.1 %copy-start.1 = (f32[2,8,240,240]{3,2,1,0:T(8,128)S(1)}, f32[2,8,240,240]{3,2,1,0:T(8,128)}, u32[]{:S(2)}) copy-start(f32[2,8,240,240]{3,2,1,0:T(8,128)} %eig_hbm.1) | copy-start | bytes 11059204
  4.2 0.7 %copy-start.6 = (s32[3,512]{1,0:T(4,128)S(1)}, s32[3,512]{1,0:T(4,128)}, u32[]{:S(2)}) copy-start(s32[3,512]{1,0:T(4,128)} %cell_ref.1) | copy-start | bytes 18436
  4.9 0.7 copy-start.7
  5.6 0.7 copy-start.8
  6.3 45.3 %copy-start.2 = (bf16[4,512,512]{2,1,0:T(8,128)(2,1)S(1)}, bf16[4,512,512]{2,1,0:T(8,128)(2,1)}, u32[]{:S(2)}) copy-start(bf16[4,512,512]{2,1,0:T(8,128)(2,1)} %constant.11.clone.dft_ref) | copy-start | bytes 6291460
  6.3 45.3 %copy-start.3 = (f32[64,512]{1,0:T(8,128)S(1)}, f32[64,512]{1,0:T(8,128)}, u32[]{:S(2)}) copy-start(f32[64,512]{1,0:T(8,128)} %constant.10.clone.sin_ref) | copy-start | bytes 393220
  6.3 45.3 %copy-start.4 = (f32[64,512]{1,0:T(8,128)S(1)}, f32[64,512]{1,0:T(8,128)}, u32[]{:S(2)}) copy-start(f32[64,512]{1,0:T(8,128)} %constant.9.clone.cos_ref) | copy-start | bytes 393220
  6.3 45.3 %copy-start.5 = (bf16[2,128,256]{2,1,0:T(8,128)(2,1)S(1)}, bf16[2,128,256]{2,1,0:T(8,128)(2,1)}, u32[]{:S(2)}) copy-start(bf16[2,128,256]{2,1,0:T(8,128)(2,1)} %constant.8.clone.low_ref) | copy-start | bytes 393220

commit v2 on v1

--- a/solution.py
+++ b/solution.py
@@ -46,8 +46,17 @@
 
 
 def project_kernel(
-    q_ref, cell_ref, mass_ref, vel_hbm, eig_hbm, out_ref, vel, eig, summed, series, vel_sem, eig_sem
+    q_hbm, cell_hbm, mass_hbm, vel_hbm, eig_hbm, out_ref,
+    q_ref, cell_ref, mass_ref, vel, eig, summed, series, small_sem, vel_sem, eig_sem,
 ):
+    small_copies = [
+        pltpu.make_async_copy(source, target, small_sem.at[n])
+        for n, (source, target) in enumerate(
+            [(q_hbm, q_ref), (cell_hbm, cell_ref), (mass_hbm, mass_ref)]
+        )
+    ]
+    for copy in small_copies:
+        copy.start()
     vel_copies = []
     for part in range(4):
         frames = pl.ds(part * 4, 4)
@@ -62,6 +71,8 @@
             copy.start()
             eig_copies.append(copy)
 
+    for copy in small_copies:
+        copy.wait()
     row = lax.broadcasted_iota(jnp.int32, (QPTS, CELLS), 0)
     products = jnp.zeros((QPTS, CELLS), jnp.int32)
     for j in range(3):
@@ -124,25 +135,28 @@
     return pl.pallas_call(
         project_kernel,
         out_shape=jax.ShapeDtypeStruct((512, 128), F32),
-        in_specs=[
-            pl.BlockSpec(memory_space=pltpu.SMEM),
-            pl.BlockSpec(memory_space=pltpu.VMEM),
-            pl.BlockSpec(memory_space=pltpu.VMEM),
-            pl.BlockSpec(memory_space=pl.ANY),
-            pl.BlockSpec(memory_space=pl.ANY),
-        ],
+        in_specs=[pl.BlockSpec(memory_space=pltpu.HBM)] * 5,
         out_specs=pl.BlockSpec(memory_space=pltpu.VMEM),
         scratch_shapes=[
+            pltpu.SMEM((3, QPTS), jnp.int32),
+            pltpu.VMEM((3, CELLS), jnp.int32),
+            pltpu.VMEM((1, DOF), F32),
             pltpu.VMEM((FRAMES, DOF, CELLS), BF16),
             pltpu.VMEM((2, QPTS, DOF, DOF), F32),
             pltpu.VMEM((2, 256, 128), F32),
             pltpu.VMEM((1928, 128), F32),
+            pltpu.SemaphoreType.DMA((3,)),
             pltpu.SemaphoreType.DMA((4,)),
             pltpu.SemaphoreType.DMA((4,)),
         ],
         compiler_params=pltpu.CompilerParams(vmem_limit_bytes=32 * 1024 * 1024),
         name="project",
-    )(q_points, cell_offsets, mass_root.reshape(1, DOF), velocities, eigvec)
+    )(
+        *[
+            pltpu.with_memory_space_constraint(operand, pltpu.HBM)
+            for operand in (q_points, cell_offsets, mass_root.reshape(1, DOF), velocities, eigvec)
+        ]
+    )
 
 
 def transform_kernel(x_ref, low_ref, cos_ref, sin_ref, dft_ref, out_ref):
@@ -177,7 +191,7 @@
     power = (real * real + imag * imag) * (1.0 / TOTAL)
     for j in range(4):
         for i in range(QUAD):
-            out_ref[pl.ds(j * 4 + i, 16, stride=16), :] = power[
+            out_ref[pl.ds(i * 4 + j, 16, stride=16), :] = power[
                 i * 16 : (i + 1) * 16, j * 128 : (j + 1) * 128
             ]
 
@@ -220,24 +234,6 @@
     )(x, *[jnp.asarray(table) for table in tables()])
 
 
-def order_kernel(x_ref, out_ref, rows):
-    for j in range(4):
-        for i in range(QUAD):
-            rows[pl.ds(i, 16, stride=QUAD), :] = x_ref[pl.ds(j * 4 + i, 16, stride=16), :]
-        out_ref[:, j * 128 : (j + 1) * 128] = rows[:PER_DEV, :]
-
-
-def order(x):
-    return pl.pallas_call(
-        order_kernel,
-        out_shape=jax.ShapeDtypeStruct((PER_DEV, SPAN), F32),
-        in_specs=[pl.BlockSpec(memory_space=pltpu.VMEM)],
-        out_specs=pl.BlockSpec(memory_space=pltpu.VMEM),
-        scratch_shapes=[pltpu.VMEM((64, 128), F32)],
-        name="order",
-    )(x)
-
-
 def per_device(velocities, mass_root, eigvec, q_points, cell_offsets):
     messages = project(velocities, mass_root, eigvec, q_points, cell_offsets)
     frames = lax.all_to_all(
@@ -245,7 +241,8 @@
     )
     power = transform(frames.reshape(512, 128))
     spectra = lax.all_to_all(power.reshape(16, 16, 128), "grp", 0, 0, tiled=True)
-    return order(spectra.reshape(256, 128))[None]
+    rows = spectra.reshape(256, 128)[: PER_DEV * 4]
+    return rows.reshape(1, PER_DEV, SPAN)
 
 
 def solution(mesh):

time: 69.8 us -> 59.6 us (0.85)
  local copies, waits for them, and re-layouts: 7.97 us -> 0.67 us
  Pallas kernels: 8.99 us -> 6.95 us
  blocking collectives: 52.4 us -> 51.7 us
    unnamed x18 -> x8, local copies, waits for them, and re-layouts: 6.3 us -> 0.02 us
    broadcast_in_dim x1 -> x0, local copies, waits for them, and re-layouts: 1.68 us -> none  [per_device(): return order(spectra.reshape(256, 128))[None]]
    pallas_call x1 -> x0, Pallas kernels: 1.63 us -> none  [order(): pl.pallas_call(order_kernel, out_shape=jax.ShapeDtypeStruct((PER_DEV, SPA...]
    all_to_all x1, blocking collectives: 13.4 us -> 12.7 us  [per_device(): lax.all_to_all(power.reshape(16, 16, 128), 'grp', 0, 0, tiled=True)]
where the time goes in v2:
time: 59.6 us; the launch traced here: 59.4 us
  blocking collectives  51.7 us (87%)
  Pallas kernels  6.95 us (12%)
  local copies, waits for them, and re-layouts  0.67 us (1%)
    all_to_all x1, blocking collectives, per_device(): lax.all_to_all(messages.reshape(512, 1, 128), ('dev', 'grp'), 0, 0, tiled...  39 us
    all_to_all x1, blocking collectives, per_device(): lax.all_to_all(power.reshape(16, 16, 128), 'grp', 0, 0, tiled=True)  12.7 us
    pallas_call x1, Pallas kernels, project(): pl.pallas_call(project_kernel, out_shape=jax.ShapeDtypeStruct((512, 128),...  5.86 us

profile of v2, /device:TPU:1, one launch (start us, length us, event | category | flops | bytes accessed | tf_op | source)
XLA Modules:
  0.0 59.4 jit_solution(12970711263082264781)
XLA Ops:
  0.0 0.0 copy-start
  0.0 0.0 copy-start.1
  0.0 0.0 copy-start.2
  0.0 0.0 copy-start.3
  0.0 5.9 %project.1 = f32[512,128]{1,0:T(8,128)S(1)} custom-call(s32[3,8]{1,0:T(4,128)} %q_hbm.1, s32[3,512]{1,0:T(4,128)} %cell_hbm.1, f32[1,240]{1,0:T(1,128)} %bitcast.10, bf16[16,240,512]{2,1,0:T(8,128)(2,1)} %vel_hbm.1, f32[2,8,240,240]{3,2,1,0:T(8,128)} %eig_hbm.1), custom_call_target="tpu_custom_call" | custom-call | tf_op jit(solution)/shard_map/project/pallas_call | solution.py:135
  5.9 39.0 %all_to_all.10 = f32[512,1,128]{2,1,0:T(1,128)S(1)} all-to-all(f32[512,1,128]{2,1,0:T(1,128)S(1)} %bitcast.7), channel_id=1, replica_groups=mesh['grp'=16,'dev'=32] {'dev','grp'}, dimensions={0} | all-to-all | bytes 524288 | tf_op jit(solution)/shard_map/all_to_all | solution.py:239
  44.9 0.0 copy-done
  44.9 0.0 copy-done.1
  44.9 0.0 copy-done.2
  44.9 0.0 copy-done.3
  44.9 1.1 %transform.1 = f32[256,128]{1,0:T(8,128)S(1)} custom-call(f32[512,128]{1,0:T(8,128)S(1)} %bitcast.8, bf16[2,128,256]{2,1,0:T(8,128)(2,1)S(1)} %copy-done.3, f32[64,512]{1,0:T(8,128)S(1)} %copy-done.2, f32[64,512]{1,0:T(8,128)S(1)} %copy-done.1, bf16[4,512,512]{2,1,0:T(8,128)(2,1)S(1)} %copy-done), custom_call_target="tpu_custom_call" | custom-call | tf_op jit(solution)/shard_map/transform/pallas_call | solution.py:227
  46.0 12.7 %all_to_all.11 = f32[16,16,128]{2,1,0:T(8,128)S(1)} all-to-all(f32[16,16,128]{2,1,0:T(8,128)S(1)} %bitcast.9), channel_id=1, replica_groups=mesh['grp'=16,'dev'=32] {'grp'}, dimensions={0} | all-to-all | bytes 262144 | tf_op jit(solution)/shard_map/all_to_all | solution.py:243
  58.7 0.7 %slice.5 = f32[15,16,128]{2,1,0:T(8,128)} slice(f32[16,16,128]{2,1,0:T(8,128)S(1)} %all_to_all.11), slice={[0:15], [0:16], [0:128]} | slice | bytes 245760 | tf_op jit(solution)/shard_map/slice | solution.py:244
Async XLA Ops:
  0.0 44.9 %copy-start = (bf16[4,512,512]{2,1,0:T(8,128)(2,1)S(1)}, bf16[4,512,512]{2,1,0:T(8,128)(2,1)}, u32[]{:S(2)}) copy-start(bf16[4,512,512]{2,1,0:T(8,128)(2,1)} %constant.11.clone.dft_ref) | copy-start | bytes 6291460
  0.0 44.9 %copy-start.1 = (f32[64,512]{1,0:T(8,128)S(1)}, f32[64,512]{1,0:T(8,128)}, u32[]{:S(2)}) copy-start(f32[64,512]{1,0:T(8,128)} %constant.10.clone.sin_ref) | copy-start | bytes 393220
  0.0 44.9 %copy-start.2 = (f32[64,512]{1,0:T(8,128)S(1)}, f32[64,512]{1,0:T(8,128)}, u32[]{:S(2)}) copy-start(f32[64,512]{1,0:T(8,128)} %constant.9.clone.cos_ref) | copy-start | bytes 393220
  0.0 44.9 %copy-start.3 = (bf16[2,128,256]{2,1,0:T(8,128)(2,1)S(1)}, bf16[2,128,256]{2,1,0:T(8,128)(2,1)}, u32[]{:S(2)}) copy-start(bf16[2,128,256]{2,1,0:T(8,128)(2,1)} %constant.8.clone.low_ref) | copy-start | bytes 393220

commit v3 on v2

--- a/solution.py
+++ b/solution.py
@@ -7,6 +7,7 @@
 from jax import lax
 from jax.experimental import pallas as pl
 from jax.experimental.pallas import tpu as pltpu
+from jax.sharding import Mesh
 from jax.sharding import PartitionSpec as P
 
 LAT = 8
@@ -20,6 +21,10 @@
 PER_DEV = 60
 QUAD = 4
 SPAN = 512
+GROUPS = np.arange(N_GRP).reshape(8, 2).T.ravel()
+VEL_PARTS = 2
+EIG_PARTS = ((0, 4), (4, 8))
+EIG_STARTS = ((0,), (1,), ())
 F32 = jnp.float32
 BF16 = jnp.bfloat16
 
@@ -58,18 +63,17 @@
     for copy in small_copies:
         copy.start()
     vel_copies = []
-    for part in range(4):
-        frames = pl.ds(part * 4, 4)
+    for part in range(VEL_PARTS):
+        frames = pl.ds(part * FRAMES // VEL_PARTS, FRAMES // VEL_PARTS)
         copy = pltpu.make_async_copy(vel_hbm.at[frames], vel.at[frames], vel_sem.at[part])
         copy.start()
         vel_copies.append(copy)
     eig_copies = []
-    for half in range(2):
-        ks = pl.ds(half * 4, 4)
-        for ri in range(2):
-            copy = pltpu.make_async_copy(eig_hbm.at[ri, ks], eig.at[ri, ks], eig_sem.at[half * 2 + ri])
-            copy.start()
-            eig_copies.append(copy)
+    for part, (low, high) in enumerate(EIG_PARTS):
+        ks = pl.ds(low, high - low)
+        eig_copies.append(pltpu.make_async_copy(eig_hbm.at[:, ks], eig.at[:, ks], eig_sem.at[part]))
+    for part in EIG_STARTS[0]:
+        eig_copies[part].start()
 
     for copy in small_copies:
         copy.wait()
@@ -86,49 +90,45 @@
     ).astype(BF16)
 
     mass = mass_ref[...]
-    for part in range(4):
-        vel_copies[part].wait()
-        for t in range(part * 4, part * 4 + 4):
-            sums = dot_t(phases, vel[t]) * mass
-            summed[0, t * 16 : (t + 1) * 16, :] = sums[:, :128]
-            summed[1, t * 16 : (t + 1) * 16, : DOF - 128] = sums[:, 128:]
-
-    series[1920:1928, :] = jnp.zeros((8, 128), F32)
-    for half in range(2):
-        first, second = [], []
-        for kk in range(4):
-            k = half * 4 + kk
-            real, imag = [
-                jnp.concatenate(
-                    [summed[lanes, pl.ds(start, 16, stride=16), :] for lanes in range(2)], axis=1
-                )[:, :DOF]
-                for start in (k, 8 + k)
-            ]
-            first += [real, imag]
-            second += [imag, -real]
-        first = jnp.concatenate(split(jnp.concatenate(first, axis=0)), axis=0)
-        second = jnp.concatenate(split(jnp.concatenate(second, axis=0)), axis=0)
-        eig_copies[half * 2].wait()
-        eig_copies[half * 2 + 1].wait()
-        for kk in range(4):
-            k = half * 4 + kk
+    for t in range(FRAMES):
+        if t % (FRAMES // VEL_PARTS) == 0:
+            vel_copies[t // (FRAMES // VEL_PARTS)].wait()
+            for part in EIG_STARTS[1 + t // (FRAMES // VEL_PARTS)]:
+                eig_copies[part].start()
+        sums = dot_t(phases, vel[t]) * mass
+        summed[0, t * 16 : (t + 1) * 16, :] = sums[:, :128]
+        summed[1, t * 16 : (t + 1) * 16, : DOF - 128] = sums[:, 128:]
+
+    series[:, DOF:, :] = jnp.zeros((QPTS, 8, 128), F32)
+    lane_quad = lax.broadcasted_iota(jnp.int32, (16, 128), 1) // 32
+    weights = []
+    for k in range(QPTS):
+        real, imag = [
+            jnp.concatenate(
+                [summed[lanes, pl.ds(start, 16, stride=16), :] for lanes in range(2)], axis=1
+            )[:, :DOF]
+            for start in (k, 8 + k)
+        ]
+        (real_hi, real_lo), (imag_hi, imag_lo) = split(real), split(imag)
+        first = jnp.concatenate([real_hi, imag_hi] * 4 + [real_lo, imag_lo] * 4, axis=0)
+        second = jnp.concatenate([imag_hi, -real_hi] * 4 + [imag_lo, -real_lo] * 4, axis=0)
+        weights.append((first, second))
+    for part, (low, high) in enumerate(EIG_PARTS):
+        eig_copies[part].wait()
+        for k in range(low, high):
+            first, second = weights[k]
             real_hi, real_lo = split(eig[0, k])
             imag_hi, imag_lo = split(eig[1, k])
             both = dot_t(real_hi, first) + dot_t(real_lo, first)
             both = both + dot_t(imag_hi, second) + dot_t(imag_lo, second)
-            series[k * DOF : (k + 1) * DOF, :] = both[:, :128] + both[:, 128:]
-
-    lane_quad = lax.broadcasted_iota(jnp.int32, (16, 128), 1) // 32
-    for chunk in range(N_DEV):
-        kk = chunk // 4 % 4
-        message = None
-        for i in range(QUAD):
-            part = series[pl.ds(chunk * PER_DEV + i, 16, stride=QUAD), :]
-            turn = (i - kk) * 32 % 128
-            if turn:
-                part = pltpu.roll(part, turn, 1)
-            message = part if message is None else jnp.where(lane_quad == i, part, message)
-        out_ref[chunk * 16 : (chunk + 1) * 16, :] = message
+            series[k, :DOF, :] = both[:, :128] + both[:, 128:]
+        for k in range(low, high):
+            for chunk in range(4):
+                message = None
+                for i in range(QUAD):
+                    rows = series[k, pl.ds(chunk * PER_DEV + i, 16, stride=QUAD), :]
+                    message = rows if message is None else jnp.where(lane_quad == i, rows, message)
+                out_ref[(4 * k + chunk) * 16 : (4 * k + chunk + 1) * 16, :] = message
 
 
 def project(velocities, mass_root, eigvec, q_points, cell_offsets):
@@ -144,10 +144,10 @@
             pltpu.VMEM((FRAMES, DOF, CELLS), BF16),
             pltpu.VMEM((2, QPTS, DOF, DOF), F32),
             pltpu.VMEM((2, 256, 128), F32),
-            pltpu.VMEM((1928, 128), F32),
+            pltpu.VMEM((QPTS, DOF + 8, 128), F32),
             pltpu.SemaphoreType.DMA((3,)),
-            pltpu.SemaphoreType.DMA((4,)),
-            pltpu.SemaphoreType.DMA((4,)),
+            pltpu.SemaphoreType.DMA((VEL_PARTS,)),
+            pltpu.SemaphoreType.DMA((len(EIG_PARTS),)),
         ],
         compiler_params=pltpu.CompilerParams(vmem_limit_bytes=32 * 1024 * 1024),
         name="project",
@@ -206,6 +206,7 @@
 def tables():
     g = np.arange(16)
     theta = 2.0 * np.pi * (g[:, None] * g[None, :] % 16) / 16
+    theta = theta[GROUPS][:, GROUPS]
     low = np.zeros((2, QUAD, 16, QUAD, 2, 16))
     for i in range(QUAD):
         low[0, i, :, i, 0] = np.cos(theta)
@@ -215,7 +216,7 @@
     hi, lo = split_np(low.reshape(128, 128))
     low = np.stack([np.concatenate([hi, hi], axis=1), np.concatenate([lo, lo], axis=1)])
     s = np.arange(SPAN)
-    twist = 2.0 * np.pi * np.tile(g[:, None] * s[None, :], (QUAD, 1)) / TOTAL
+    twist = 2.0 * np.pi * np.tile(GROUPS[:, None] * s[None, :], (QUAD, 1)) / TOTAL
     full = 2.0 * np.pi * (s[:, None] * s[None, :] % SPAN) / SPAN
     cos_hi, cos_lo = split_np(np.cos(full))
     sin_hi, sin_lo = split_np(np.sin(full))
@@ -237,19 +238,23 @@
 def per_device(velocities, mass_root, eigvec, q_points, cell_offsets):
     messages = project(velocities, mass_root, eigvec, q_points, cell_offsets)
     frames = lax.all_to_all(
-        messages.reshape(512, 1, 128), ("dev", "grp"), 0, 0, tiled=True
+        messages.reshape(512, 1, 128), ("dev", "grp_x", "grp_y"), 0, 0, tiled=True
     )
     power = transform(frames.reshape(512, 128))
-    spectra = lax.all_to_all(power.reshape(16, 16, 128), "grp", 0, 0, tiled=True)
+    spectra = lax.all_to_all(
+        power.reshape(16, 16, 128), ("grp_x", "grp_y"), 0, 0, tiled=True
+    )
     rows = spectra.reshape(256, 128)[: PER_DEV * 4]
     return rows.reshape(1, PER_DEV, SPAN)
 
 
 def solution(mesh):
+    split_mesh = Mesh(mesh.devices.reshape(8, 2, N_DEV), ("grp_y", "grp_x", "dev"))
+    grp = ("grp_y", "grp_x")
     return jax.shard_map(
         per_device,
-        mesh=mesh,
-        in_specs=(P(("grp", "dev"), None, None), P(), P(), P(), P()),
-        out_specs=P("grp", "dev", None),
+        mesh=split_mesh,
+        in_specs=(P(grp + ("dev",), None, None), P(), P(), P(), P()),
+        out_specs=P(grp, "dev", None),
         check_vma=False,
     )

time: 59.6 us -> 58.1 us (0.975)
  blocking collectives: 51.7 us -> 50.8 us
  Pallas kernels: 6.95 us -> 6.23 us
    all_to_all x2, blocking collectives: 51.7 us -> 50.8 us  [the longest x1 39.3 us: per_device(): lax.all_to_all(messages.reshape(512, 1, 128), ('dev', 'grp_x', 'grp_y'),...]
    pallas_call x1, Pallas kernels: 5.86 us -> 5.14 us  [project(): pl.pallas_call(project_kernel, out_shape=jax.ShapeDtypeStruct((512, 128),...]
where the time goes in v3:
time: 58.1 us; the launch traced here: 57.7 us
  blocking collectives  50.8 us (87%)
  Pallas kernels  6.23 us (11%)
  local copies, waits for them, and re-layouts  0.67 us (1%)
    all_to_all x1, blocking collectives, per_device(): lax.all_to_all(messages.reshape(512, 1, 128), ('dev', 'grp_x', 'grp_y'),...  39.3 us
    all_to_all x1, blocking collectives, per_device(): lax.all_to_all(power.reshape(16, 16, 128), ('grp_x', 'grp_y'), 0, 0, tile...  11.5 us
    pallas_call x1, Pallas kernels, project(): pl.pallas_call(project_kernel, out_shape=jax.ShapeDtypeStruct((512, 128),...  5.14 us

profile of v3, /device:TPU:1, one launch (start us, length us, event | category | flops | bytes accessed | tf_op | source)
XLA Modules:
  0.0 57.7 jit_solution(6885444277574632303)
XLA Ops:
  0.0 0.0 copy-start
  0.0 0.0 copy-start.1
  0.0 0.0 copy-start.2
  0.0 0.0 copy-start.3
  0.0 5.1 %project.1 = f32[512,128]{1,0:T(8,128)S(1)} custom-call(s32[3,8]{1,0:T(4,128)} %q_hbm.1, s32[3,512]{1,0:T(4,128)} %cell_hbm.1, f32[1,240]{1,0:T(1,128)} %bitcast.10, bf16[16,240,512]{2,1,0:T(8,128)(2,1)} %vel_hbm.1, f32[2,8,240,240]{3,2,1,0:T(8,128)} %eig_hbm.1), custom_call_target="tpu_custom_call" | custom-call | tf_op jit(solution)/shard_map/project/pallas_call | solution.py:135
  5.2 39.3 %all_to_all.10 = f32[512,1,128]{2,1,0:T(1,128)S(1)} all-to-all(f32[512,1,128]{2,1,0:T(1,128)S(1)} %bitcast.7), channel_id=1, replica_groups=mesh['grp_y'=8,'grp_x'=2,'dev'=32] {'dev','grp_x','grp_y'}, dimensions={0} | all-to-all | bytes 524288 | tf_op jit(solution)/shard_map/all_to_all | solution.py:240
  44.4 0.0 copy-done
  44.4 0.0 copy-done.1
  44.4 0.0 copy-done.2
  44.4 0.0 copy-done.3
  44.4 1.1 %transform.1 = f32[256,128]{1,0:T(8,128)S(1)} custom-call(f32[512,128]{1,0:T(8,128)S(1)} %bitcast.8, bf16[2,128,256]{2,1,0:T(8,128)(2,1)S(1)} %copy-done.3, f32[64,512]{1,0:T(8,128)S(1)} %copy-done.2, f32[64,512]{1,0:T(8,128)S(1)} %copy-done.1, bf16[4,512,512]{2,1,0:T(8,128)(2,1)S(1)} %copy-done), custom_call_target="tpu_custom_call" | custom-call | tf_op jit(solution)/shard_map/transform/pallas_call | solution.py:228
  45.5 11.5 %all_to_all.11 = f32[16,16,128]{2,1,0:T(8,128)S(1)} all-to-all(f32[16,16,128]{2,1,0:T(8,128)S(1)} %bitcast.9), channel_id=1, replica_groups=mesh['grp_y'=8,'grp_x'=2,'dev'=32] {'grp_x','grp_y'}, dimensions={0} | all-to-all | bytes 262144 | tf_op jit(solution)/shard_map/all_to_all | solution.py:244
  57.1 0.7 %slice.5 = f32[15,16,128]{2,1,0:T(8,128)} slice(f32[16,16,128]{2,1,0:T(8,128)S(1)} %all_to_all.11), slice={[0:15], [0:16], [0:128]} | slice | bytes 245760 | tf_op jit(solution)/shard_map/slice | solution.py:247
Async XLA Ops:
  0.0 44.4 %copy-start = (bf16[4,512,512]{2,1,0:T(8,128)(2,1)S(1)}, bf16[4,512,512]{2,1,0:T(8,128)(2,1)}, u32[]{:S(2)}) copy-start(bf16[4,512,512]{2,1,0:T(8,128)(2,1)} %constant.11.clone.dft_ref) | copy-start | bytes 6291460
  0.0 44.4 %copy-start.1 = (f32[64,512]{1,0:T(8,128)S(1)}, f32[64,512]{1,0:T(8,128)}, u32[]{:S(2)}) copy-start(f32[64,512]{1,0:T(8,128)} %constant.10.clone.sin_ref) | copy-start | bytes 393220
  0.0 44.4 %copy-start.2 = (f32[64,512]{1,0:T(8,128)S(1)}, f32[64,512]{1,0:T(8,128)}, u32[]{:S(2)}) copy-start(f32[64,512]{1,0:T(8,128)} %constant.9.clone.cos_ref) | copy-start | bytes 393220
  0.0 44.4 %copy-start.3 = (bf16[2,128,256]{2,1,0:T(8,128)(2,1)S(1)}, bf16[2,128,256]{2,1,0:T(8,128)(2,1)}, u32[]{:S(2)}) copy-start(bf16[2,128,256]{2,1,0:T(8,128)(2,1)} %constant.8.clone.low_ref) | copy-start | bytes 393220

commit v4 on v3

--- a/solution.py
+++ b/solution.py
@@ -96,8 +96,9 @@
             for part in EIG_STARTS[1 + t // (FRAMES // VEL_PARTS)]:
                 eig_copies[part].start()
         sums = dot_t(phases, vel[t]) * mass
-        summed[0, t * 16 : (t + 1) * 16, :] = sums[:, :128]
-        summed[1, t * 16 : (t + 1) * 16, : DOF - 128] = sums[:, 128:]
+        at = (t % 2 * 8 + t // 2) * 16
+        summed[0, at : at + 16, :] = sums[:, :128]
+        summed[1, at : at + 16, : DOF - 128] = sums[:, 128:]
 
     series[:, DOF:, :] = jnp.zeros((QPTS, 8, 128), F32)
     lane_quad = lax.broadcasted_iota(jnp.int32, (16, 128), 1) // 32
@@ -119,9 +120,9 @@
             first, second = weights[k]
             real_hi, real_lo = split(eig[0, k])
             imag_hi, imag_lo = split(eig[1, k])
-            both = dot_t(real_hi, first) + dot_t(real_lo, first)
-            both = both + dot_t(imag_hi, second) + dot_t(imag_lo, second)
-            series[k, :DOF, :] = both[:, :128] + both[:, 128:]
+            both = dot_t(jnp.concatenate([real_hi, real_lo], axis=0), first)
+            both = both + dot_t(jnp.concatenate([imag_hi, imag_lo], axis=0), second)
+            series[k, :DOF, :] = (both[:DOF, :128] + both[:DOF, 128:]) + both[DOF:, :128]
         for k in range(low, high):
             for chunk in range(4):
                 message = None
@@ -159,41 +160,57 @@
     )
 
 
-def transform_kernel(x_ref, low_ref, cos_ref, sin_ref, dft_ref, out_ref):
+def transform_kernel(x_ref, low_ref, twist_ref, dft_ref, turn_ref, out_ref):
     lane = lax.broadcasted_iota(jnp.int32, (16, 128), 1)
     tiles = []
-    for j in range(4):
-        blocks = [x_ref[(8 * j + d) * 16 : (8 * j + d + 1) * 16, :] for d in range(8)]
-        for bit in (4, 2, 1):
-            width = bit * 16
+    for j in range(2):
+        blocks = [x_ref[(16 * j + d) * 16 : (16 * j + d + 1) * 16, :] for d in range(16)]
+        for bit in (8, 4, 2, 1):
+            width = bit * 8
             keep = (lane & width) == 0
-            for a in range(8):
+            for a in range(16):
                 if a & bit:
                     continue
                 b = a | bit
                 u, v = blocks[a], blocks[b]
                 blocks[a] = jnp.where(keep, u, pltpu.roll(v, width, 1))
                 blocks[b] = jnp.where(keep, pltpu.roll(u, 128 - width, 1), v)
-        tiles.append(jnp.concatenate(blocks, axis=0))
-    gathered = jnp.concatenate(tiles, axis=1)
-    stacked = jnp.concatenate(split(gathered), axis=0)
-    low = dot(low_ref[0], stacked) + dot(low_ref[1], stacked)
-    real, imag = low[:64], low[64:]
-    cosine, sine = cos_ref[...], sin_ref[...]
-    turned = jnp.concatenate(
-        [real * cosine + imag * sine, imag * cosine - real * sine], axis=0
-    )
-    hi, lo = split(turned)
-    by_cos = dot(hi, dft_ref[0]) + dot(lo, dft_ref[0]) + dot(hi, dft_ref[2])
-    by_sin = dot(hi, dft_ref[1]) + dot(lo, dft_ref[1]) + dot(hi, dft_ref[3])
-    real = by_cos[:64] + by_sin[64:]
-    imag = by_cos[64:] - by_sin[:64]
-    power = (real * real + imag * imag) * (1.0 / TOTAL)
-    for j in range(4):
-        for i in range(QUAD):
-            out_ref[pl.ds(i * 4 + j, 16, stride=16), :] = power[
-                i * 16 : (i + 1) * 16, j * 128 : (j + 1) * 128
-            ]
+        tiles.append(blocks)
+    halves = []
+    for parity in range(2):
+        gathered = jnp.concatenate(
+            [jnp.concatenate(blocks[parity::2], axis=0) for blocks in tiles], axis=1
+        )
+        stacked = jnp.concatenate(split(gathered), axis=0)
+        low = dot(low_ref[0], stacked) + dot(low_ref[1], stacked)
+        real, imag = low[:64], low[64:]
+        cosine, sine = [
+            jnp.concatenate([twist_ref[2 * parity + part]] * QUAD, axis=0) for part in range(2)
+        ]
+        halves += [real * cosine + imag * sine, imag * cosine - real * sine]
+    hi, lo = split(jnp.concatenate(halves, axis=0))
+    stacked = jnp.concatenate([hi, lo], axis=0)
+    by_cos = dot(stacked, dft_ref[0])
+    by_sin = dot(stacked, dft_ref[1])
+    by_cos = by_cos[:256] + by_cos[256:] + dot(hi, dft_ref[2])
+    by_sin = by_sin[:256] + by_sin[256:] + dot(hi, dft_ref[3])
+    even_real = by_cos[:64] + by_sin[64:128]
+    even_imag = by_cos[64:128] - by_sin[:64]
+    real = by_cos[128:192] + by_sin[192:]
+    imag = by_cos[192:] - by_sin[128:192]
+    cosine, sine = turn_ref[0:1, :], turn_ref[1:2, :]
+    odd_real = real * cosine + imag * sine
+    odd_imag = imag * cosine - real * sine
+    for half in range(2):
+        if half:
+            odd_real, odd_imag = -odd_real, -odd_imag
+        real, imag = even_real + odd_real, even_imag + odd_imag
+        power = (real * real + imag * imag) * (1.0 / TOTAL)
+        for j in range(2):
+            for i in range(QUAD):
+                out_ref[pl.ds(i * 4 + half * 2 + j, 16, stride=16), :] = power[
+                    i * 16 : (i + 1) * 16, j * 128 : (j + 1) * 128
+                ]
 
 
 def split_np(x):
@@ -215,13 +232,17 @@
         low[1, i, :, i, 1] = np.cos(theta)
     hi, lo = split_np(low.reshape(128, 128))
     low = np.stack([np.concatenate([hi, hi], axis=1), np.concatenate([lo, lo], axis=1)])
-    s = np.arange(SPAN)
-    twist = 2.0 * np.pi * np.tile(GROUPS[:, None] * s[None, :], (QUAD, 1)) / TOTAL
-    full = 2.0 * np.pi * (s[:, None] * s[None, :] % SPAN) / SPAN
+    n = np.arange(SPAN // 2)
+    s = np.stack([2 * n, 2 * n + 1])
+    twist = 2.0 * np.pi * GROUPS[:, None] * s[:, None, :] / TOTAL
+    twist = np.stack([np.cos(twist), np.sin(twist)], axis=1).reshape(4, 16, SPAN // 2)
+    full = 2.0 * np.pi * (n[:, None] * n[None, :] % 256) / 256
     cos_hi, cos_lo = split_np(np.cos(full))
     sin_hi, sin_lo = split_np(np.sin(full))
     dft = np.stack([cos_hi, sin_hi, cos_lo, sin_lo])
-    return low, np.cos(twist).astype(np.float32), np.sin(twist).astype(np.float32), dft
+    turn = 2.0 * np.pi * n / SPAN
+    turn = np.stack([np.cos(turn), np.sin(turn)]).astype(np.float32)
+    return low, twist.astype(np.float32), dft, turn
 
 
 def transform(x):

time: 58.1 us -> 57.5 us (0.990)
  Pallas kernels: 6.23 us -> 5.55 us
where the time goes in v4:
time: 57.5 us; the launch traced here: 57 us
  blocking collectives  50.8 us (88%)
  Pallas kernels  5.55 us (10%)
  local copies, waits for them, and re-layouts  0.67 us (1%)
    all_to_all x1, blocking collectives, per_device(): lax.all_to_all(messages.reshape(512, 1, 128), ('dev', 'grp_x', 'grp_y'),...  39.3 us
    all_to_all x1, blocking collectives, per_device(): lax.all_to_all(power.reshape(16, 16, 128), ('grp_x', 'grp_y'), 0, 0, tile...  11.5 us
    pallas_call x1, Pallas kernels, project(): pl.pallas_call(project_kernel, out_shape=jax.ShapeDtypeStruct((512, 128),...  4.59 us

profile of v4, /device:TPU:1, one launch (start us, length us, event | category | flops | bytes accessed | tf_op | source)
XLA Modules:
  0.0 57.0 jit_solution(16319153964857783381)
XLA Ops:
  0.0 0.0 copy-start
  0.0 0.0 copy-start.1
  0.0 0.0 copy-start.2
  0.0 0.0 copy-start.3
  0.0 4.6 %project.1 = f32[512,128]{1,0:T(8,128)S(1)} custom-call(s32[3,8]{1,0:T(4,128)} %q_hbm.1, s32[3,512]{1,0:T(4,128)} %cell_hbm.1, f32[1,240]{1,0:T(1,128)} %bitcast.10, bf16[16,240,512]{2,1,0:T(8,128)(2,1)} %vel_hbm.1, f32[2,8,240,240]{3,2,1,0:T(8,128)} %eig_hbm.1), custom_call_target="tpu_custom_call" | custom-call | tf_op jit(solution)/shard_map/project/pallas_call | solution.py:136
  4.6 39.3 %all_to_all.10 = f32[512,1,128]{2,1,0:T(1,128)S(1)} all-to-all(f32[512,1,128]{2,1,0:T(1,128)S(1)} %bitcast.8), channel_id=1, replica_groups=mesh['grp_y'=8,'grp_x'=2,'dev'=32] {'dev','grp_x','grp_y'}, dimensions={0} | all-to-all | bytes 524288 | tf_op jit(solution)/shard_map/all_to_all | solution.py:261
  43.9 0.0 copy-done
  43.9 0.0 copy-done.1
  43.9 0.0 copy-done.2
  43.9 0.0 copy-done.3
  43.9 1.0 %transform.1 = f32[256,128]{1,0:T(8,128)S(1)} custom-call(f32[512,128]{1,0:T(8,128)S(1)} %bitcast.7, bf16[2,128,256]{2,1,0:T(8,128)(2,1)S(1)} %copy-done.1, f32[4,16,256]{2,1,0:T(8,128)S(1)} %copy-done.2, bf16[4,256,256]{2,1,0:T(8,128)(2,1)S(1)} %copy-done, f32[2,256]{1,0:T(2,128)S(1)} %copy-done.3), custom_call_target="tpu_custom_call" | custom-call | tf_op jit(solution)/shard_map/transform/pallas_call | solution.py:249
  44.9 11.5 %all_to_all.11 = f32[16,16,128]{2,1,0:T(8,128)S(1)} all-to-all(f32[16,16,128]{2,1,0:T(8,128)S(1)} %bitcast.9), channel_id=1, replica_groups=mesh['grp_y'=8,'grp_x'=2,'dev'=32] {'grp_x','grp_y'}, dimensions={0} | all-to-all | bytes 262144 | tf_op jit(solution)/shard_map/all_to_all | solution.py:265
  56.4 0.7 %slice.5 = f32[15,16,128]{2,1,0:T(8,128)} slice(f32[16,16,128]{2,1,0:T(8,128)S(1)} %all_to_all.11), slice={[0:15], [0:16], [0:128]} | slice | bytes 245760 | tf_op jit(solution)/shard_map/slice | solution.py:268
Async XLA Ops:
  0.0 43.9 %copy-start = (bf16[4,256,256]{2,1,0:T(8,128)(2,1)S(1)}, bf16[4,256,256]{2,1,0:T(8,128)(2,1)}, u32[]{:S(2)}) copy-start(bf16[4,256,256]{2,1,0:T(8,128)(2,1)} %constant.10.clone.dft_ref) | copy-start | bytes 1572868
  0.0 43.9 %copy-start.1 = (bf16[2,128,256]{2,1,0:T(8,128)(2,1)S(1)}, bf16[2,128,256]{2,1,0:T(8,128)(2,1)}, u32[]{:S(2)}) copy-start(bf16[2,128,256]{2,1,0:T(8,128)(2,1)} %constant.8.clone.low_ref) | copy-start | bytes 393220
  0.0 43.9 %copy-start.2 = (f32[4,16,256]{2,1,0:T(8,128)S(1)}, f32[4,16,256]{2,1,0:T(8,128)}, u32[]{:S(2)}) copy-start(f32[4,16,256]{2,1,0:T(8,128)} %constant.9.clone.twist_ref) | copy-start | bytes 196612
  0.0 43.9 %copy-start.3 = (f32[2,256]{1,0:T(2,128)S(1)}, f32[2,256]{1,0:T(2,128)}, u32[]{:S(2)}) copy-start(f32[2,256]{1,0:T(2,128)} %constant.11.clone.turn_ref) | copy-start | bytes 6148

commit v5 on v4

--- a/solution.py
+++ b/solution.py
@@ -96,7 +96,7 @@
             for part in EIG_STARTS[1 + t // (FRAMES // VEL_PARTS)]:
                 eig_copies[part].start()
         sums = dot_t(phases, vel[t]) * mass
-        at = (t % 2 * 8 + t // 2) * 16
+        at = (t % 4 * 4 + t // 4) * 16
         summed[0, at : at + 16, :] = sums[:, :128]
         summed[1, at : at + 16, : DOF - 128] = sums[:, 128:]
 
@@ -161,56 +161,52 @@
 
 
 def transform_kernel(x_ref, low_ref, twist_ref, dft_ref, turn_ref, out_ref):
-    lane = lax.broadcasted_iota(jnp.int32, (16, 128), 1)
-    tiles = []
-    for j in range(2):
-        blocks = [x_ref[(16 * j + d) * 16 : (16 * j + d + 1) * 16, :] for d in range(16)]
-        for bit in (8, 4, 2, 1):
-            width = bit * 8
-            keep = (lane & width) == 0
-            for a in range(16):
-                if a & bit:
-                    continue
-                b = a | bit
-                u, v = blocks[a], blocks[b]
-                blocks[a] = jnp.where(keep, u, pltpu.roll(v, width, 1))
-                blocks[b] = jnp.where(keep, pltpu.roll(u, 128 - width, 1), v)
-        tiles.append(blocks)
-    halves = []
-    for parity in range(2):
-        gathered = jnp.concatenate(
-            [jnp.concatenate(blocks[parity::2], axis=0) for blocks in tiles], axis=1
-        )
+    block = lax.broadcasted_iota(jnp.int32, (16, 128), 1) // 4
+    rows = [x_ref[d * 16 : (d + 1) * 16, :] for d in range(32)]
+    rows = [pltpu.roll(row, 4 * d, 1) if d else row for d, row in enumerate(rows)]
+    for bit in (1, 2, 4, 8, 16):
+        moves = (block & bit) != 0
+        rows = [jnp.where(moves, rows[(d + bit) % 32], rows[d]) for d in range(32)]
+    rows = [rows[-n % 32] for n in range(32)]
+    rows = [pltpu.roll(row, 128 - 4 * n, 1) if n else row for n, row in enumerate(rows)]
+    parts = []
+    for residue in range(4):
+        gathered = jnp.concatenate(rows[residue::4], axis=0)
         stacked = jnp.concatenate(split(gathered), axis=0)
         low = dot(low_ref[0], stacked) + dot(low_ref[1], stacked)
         real, imag = low[:64], low[64:]
         cosine, sine = [
-            jnp.concatenate([twist_ref[2 * parity + part]] * QUAD, axis=0) for part in range(2)
+            jnp.concatenate([twist_ref[2 * residue + part]] * QUAD, axis=0) for part in range(2)
         ]
-        halves += [real * cosine + imag * sine, imag * cosine - real * sine]
-    hi, lo = split(jnp.concatenate(halves, axis=0))
-    stacked = jnp.concatenate([hi, lo], axis=0)
-    by_cos = dot(stacked, dft_ref[0])
-    by_sin = dot(stacked, dft_ref[1])
-    by_cos = by_cos[:256] + by_cos[256:] + dot(hi, dft_ref[2])
-    by_sin = by_sin[:256] + by_sin[256:] + dot(hi, dft_ref[3])
-    even_real = by_cos[:64] + by_sin[64:128]
-    even_imag = by_cos[64:128] - by_sin[:64]
-    real = by_cos[128:192] + by_sin[192:]
-    imag = by_cos[192:] - by_sin[128:192]
-    cosine, sine = turn_ref[0:1, :], turn_ref[1:2, :]
-    odd_real = real * cosine + imag * sine
-    odd_imag = imag * cosine - real * sine
-    for half in range(2):
-        if half:
-            odd_real, odd_imag = -odd_real, -odd_imag
-        real, imag = even_real + odd_real, even_imag + odd_imag
-        power = (real * real + imag * imag) * (1.0 / TOTAL)
-        for j in range(2):
-            for i in range(QUAD):
-                out_ref[pl.ds(i * 4 + half * 2 + j, 16, stride=16), :] = power[
-                    i * 16 : (i + 1) * 16, j * 128 : (j + 1) * 128
-                ]
+        parts += [real * cosine + imag * sine, imag * cosine - real * sine]
+    both = jnp.concatenate(split(jnp.concatenate(parts, axis=0)), axis=1)
+    both = dot(both, dft_ref[0]) + dot(both, dft_ref[1])
+    real, imag = [], []
+    for residue in range(4):
+        upper = both[residue * 128 : residue * 128 + 64]
+        lower = both[residue * 128 + 64 : residue * 128 + 128]
+        a = upper[:, :128] + lower[:, 128:]
+        b = lower[:, :128] - upper[:, 128:]
+        if residue:
+            cosine = turn_ref[2 * residue : 2 * residue + 1, :]
+            sine = turn_ref[2 * residue + 1 : 2 * residue + 2, :]
+            a, b = a * cosine + b * sine, b * cosine - a * sine
+        real.append(a)
+        imag.append(b)
+    sum_real, sum_imag = real[0] + real[2], imag[0] + imag[2]
+    gap_real, gap_imag = real[0] - real[2], imag[0] - imag[2]
+    odd_real, odd_imag = real[1] + real[3], imag[1] + imag[3]
+    far_real, far_imag = real[1] - real[3], imag[1] - imag[3]
+    quarters = [
+        (sum_real + odd_real, sum_imag + odd_imag),
+        (gap_real + far_imag, gap_imag - far_real),
+        (sum_real - odd_real, sum_imag - odd_imag),
+        (gap_real - far_imag, gap_imag + far_real),
+    ]
+    for j, (a, b) in enumerate(quarters):
+        power = (a * a + b * b) * (1.0 / TOTAL)
+        for i in range(QUAD):
+            out_ref[pl.ds(i * 4 + j, 16, stride=16), :] = power[i * 16 : (i + 1) * 16, :]
 
 
 def split_np(x):
@@ -232,17 +228,17 @@
         low[1, i, :, i, 1] = np.cos(theta)
     hi, lo = split_np(low.reshape(128, 128))
     low = np.stack([np.concatenate([hi, hi], axis=1), np.concatenate([lo, lo], axis=1)])
-    n = np.arange(SPAN // 2)
-    s = np.stack([2 * n, 2 * n + 1])
+    n = np.arange(SPAN // 4)
+    residue = np.arange(4)
+    s = 4 * n[None, :] + residue[:, None]
     twist = 2.0 * np.pi * GROUPS[:, None] * s[:, None, :] / TOTAL
-    twist = np.stack([np.cos(twist), np.sin(twist)], axis=1).reshape(4, 16, SPAN // 2)
-    full = 2.0 * np.pi * (n[:, None] * n[None, :] % 256) / 256
-    cos_hi, cos_lo = split_np(np.cos(full))
-    sin_hi, sin_lo = split_np(np.sin(full))
-    dft = np.stack([cos_hi, sin_hi, cos_lo, sin_lo])
-    turn = 2.0 * np.pi * n / SPAN
-    turn = np.stack([np.cos(turn), np.sin(turn)]).astype(np.float32)
-    return low, twist.astype(np.float32), dft, turn
+    twist = np.stack([np.cos(twist), np.sin(twist)], axis=1).reshape(8, 16, SPAN // 4)
+    full = 2.0 * np.pi * (n[:, None] * n[None, :] % 128) / 128
+    hi, lo = split_np(np.concatenate([np.cos(full), np.sin(full)], axis=1))
+    dft = np.stack([np.concatenate([hi, hi], axis=0), np.concatenate([lo, np.zeros_like(lo)], axis=0)])
+    turn = 2.0 * np.pi * residue[:, None] * n / SPAN
+    turn = np.stack([np.cos(turn), np.sin(turn)], axis=1).reshape(8, SPAN // 4)
+    return low, twist.astype(np.float32), dft, turn.astype(np.float32)
 
 
 def transform(x):

time: 57.5 us -> 57.1 us (level)
  no operation moved by 1% of the time
where the time goes in v5:
time: 57.1 us; the launch traced here: 56.7 us
  blocking collectives  50.8 us (89%)
  Pallas kernels  5.22 us (9%)
  local copies, waits for them, and re-layouts  0.67 us (1%)
    all_to_all x1, blocking collectives, per_device(): lax.all_to_all(messages.reshape(512, 1, 128), ('dev', 'grp_x', 'grp_y'),...  39.3 us
    all_to_all x1, blocking collectives, per_device(): lax.all_to_all(power.reshape(16, 16, 128), ('grp_x', 'grp_y'), 0, 0, tile...  11.5 us
    pallas_call x1, Pallas kernels, project(): pl.pallas_call(project_kernel, out_shape=jax.ShapeDtypeStruct((512, 128),...  4.55 us

profile of v5, /device:TPU:1, one launch (start us, length us, event | category | flops | bytes accessed | tf_op | source)
XLA Modules:
  0.0 56.7 jit_solution(2148781273588324847)
XLA Ops:
  0.0 0.0 copy-start
  0.0 0.0 copy-start.1
  0.0 0.0 copy-start.2
  0.0 0.0 copy-start.3
  0.0 4.5 %project.1 = f32[512,128]{1,0:T(8,128)S(1)} custom-call(s32[3,8]{1,0:T(4,128)} %q_hbm.1, s32[3,512]{1,0:T(4,128)} %cell_hbm.1, f32[1,240]{1,0:T(1,128)} %bitcast.10, bf16[16,240,512]{2,1,0:T(8,128)(2,1)} %vel_hbm.1, f32[2,8,240,240]{3,2,1,0:T(8,128)} %eig_hbm.1), custom_call_target="tpu_custom_call" | custom-call | tf_op jit(solution)/shard_map/project/pallas_call | solution.py:136
  4.6 39.3 %all_to_all.10 = f32[512,1,128]{2,1,0:T(1,128)S(1)} all-to-all(f32[512,1,128]{2,1,0:T(1,128)S(1)} %bitcast.7), channel_id=1, replica_groups=mesh['grp_y'=8,'grp_x'=2,'dev'=32] {'dev','grp_x','grp_y'}, dimensions={0} | all-to-all | bytes 524288 | tf_op jit(solution)/shard_map/all_to_all | solution.py:257
  43.8 0.0 copy-done
  43.8 0.0 copy-done.1
  43.8 0.0 copy-done.2
  43.8 0.0 copy-done.3
  43.8 0.7 %transform.1 = f32[256,128]{1,0:T(8,128)S(1)} custom-call(f32[512,128]{1,0:T(8,128)S(1)} %bitcast.8, bf16[2,128,256]{2,1,0:T(8,128)(2,1)S(1)} %copy-done.1, f32[8,16,128]{2,1,0:T(8,128)S(1)} %copy-done.2, bf16[2,256,256]{2,1,0:T(8,128)(2,1)S(1)} %copy-done, f32[8,128]{1,0:T(8,128)S(1)} %copy-done.3), custom_call_target="tpu_custom_call" | custom-call | tf_op jit(solution)/shard_map/transform/pallas_call | solution.py:245
  44.5 11.5 %all_to_all.11 = f32[16,16,128]{2,1,0:T(8,128)S(1)} all-to-all(f32[16,16,128]{2,1,0:T(8,128)S(1)} %bitcast.9), channel_id=1, replica_groups=mesh['grp_y'=8,'grp_x'=2,'dev'=32] {'grp_x','grp_y'}, dimensions={0} | all-to-all | bytes 262144 | tf_op jit(solution)/shard_map/all_to_all | solution.py:261
  56.0 0.7 %slice.5 = f32[15,16,128]{2,1,0:T(8,128)} slice(f32[16,16,128]{2,1,0:T(8,128)S(1)} %all_to_all.11), slice={[0:15], [0:16], [0:128]} | slice | bytes 245760 | tf_op jit(solution)/shard_map/slice | solution.py:264
Async XLA Ops:
  0.0 43.8 %copy-start = (bf16[2,256,256]{2,1,0:T(8,128)(2,1)S(1)}, bf16[2,256,256]{2,1,0:T(8,128)(2,1)}, u32[]{:S(2)}) copy-start(bf16[2,256,256]{2,1,0:T(8,128)(2,1)} %constant.10.clone.dft_ref) | copy-start | bytes 786436
  0.0 43.8 %copy-start.1 = (bf16[2,128,256]{2,1,0:T(8,128)(2,1)S(1)}, bf16[2,128,256]{2,1,0:T(8,128)(2,1)}, u32[]{:S(2)}) copy-start(bf16[2,128,256]{2,1,0:T(8,128)(2,1)} %constant.8.clone.low_ref) | copy-start | bytes 393220
  0.0 43.8 %copy-start.2 = (f32[8,16,128]{2,1,0:T(8,128)S(1)}, f32[8,16,128]{2,1,0:T(8,128)}, u32[]{:S(2)}) copy-start(f32[8,16,128]{2,1,0:T(8,128)} %constant.9.clone.twist_ref) | copy-start | bytes 196612
  0.0 43.8 %copy-start.3 = (f32[8,128]{1,0:T(8,128)S(1)}, f32[8,128]{1,0:T(8,128)}, u32[]{:S(2)}) copy-start(f32[8,128]{1,0:T(8,128)} %constant.11.clone.turn_ref) | copy-start | bytes 12292

commit v6 on v5

--- a/solution.py
+++ b/solution.py
@@ -169,18 +169,20 @@
         rows = [jnp.where(moves, rows[(d + bit) % 32], rows[d]) for d in range(32)]
     rows = [rows[-n % 32] for n in range(32)]
     rows = [pltpu.roll(row, 128 - 4 * n, 1) if n else row for n, row in enumerate(rows)]
+    low_hi = jnp.concatenate([low_ref[0]] * 2, axis=1)
     parts = []
     for residue in range(4):
         gathered = jnp.concatenate(rows[residue::4], axis=0)
-        stacked = jnp.concatenate(split(gathered), axis=0)
-        low = dot(low_ref[0], stacked) + dot(low_ref[1], stacked)
+        hi, lo = split(gathered)
+        low = dot(low_hi, jnp.concatenate([hi, lo], axis=0)) + dot(low_ref[1], hi)
         real, imag = low[:64], low[64:]
         cosine, sine = [
             jnp.concatenate([twist_ref[2 * residue + part]] * QUAD, axis=0) for part in range(2)
         ]
         parts += [real * cosine + imag * sine, imag * cosine - real * sine]
-    both = jnp.concatenate(split(jnp.concatenate(parts, axis=0)), axis=1)
-    both = dot(both, dft_ref[0]) + dot(both, dft_ref[1])
+    hi, lo = split(jnp.concatenate(parts, axis=0))
+    both = dot(jnp.concatenate([hi, lo], axis=1), jnp.concatenate([dft_ref[0]] * 2, axis=0))
+    both = both + dot(hi, dft_ref[1])
     real, imag = [], []
     for residue in range(4):
         upper = both[residue * 128 : residue * 128 + 64]
@@ -227,7 +229,7 @@
         low[1, i, :, i, 0] = -np.sin(theta)
         low[1, i, :, i, 1] = np.cos(theta)
     hi, lo = split_np(low.reshape(128, 128))
-    low = np.stack([np.concatenate([hi, hi], axis=1), np.concatenate([lo, lo], axis=1)])
+    low = np.stack([hi, lo])
     n = np.arange(SPAN // 4)
     residue = np.arange(4)
     s = 4 * n[None, :] + residue[:, None]
@@ -235,7 +237,7 @@
     twist = np.stack([np.cos(twist), np.sin(twist)], axis=1).reshape(8, 16, SPAN // 4)
     full = 2.0 * np.pi * (n[:, None] * n[None, :] % 128) / 128
     hi, lo = split_np(np.concatenate([np.cos(full), np.sin(full)], axis=1))
-    dft = np.stack([np.concatenate([hi, hi], axis=0), np.concatenate([lo, np.zeros_like(lo)], axis=0)])
+    dft = np.stack([hi, lo])
     turn = 2.0 * np.pi * residue[:, None] * n / SPAN
     turn = np.stack([np.cos(turn), np.sin(turn)], axis=1).reshape(8, SPAN // 4)
     return low, twist.astype(np.float32), dft, turn.astype(np.float32)

time: 57.1 us -> 57.1 us (level)
  no operation moved by 1% of the time
where the time goes in v6:
time: 57.1 us; the launch traced here: 56.7 us
  blocking collectives  50.8 us (89%)
  Pallas kernels  5.22 us (9%)
  local copies, waits for them, and re-layouts  0.67 us (1%)
    all_to_all x1, blocking collectives, per_device(): lax.all_to_all(messages.reshape(512, 1, 128), ('dev', 'grp_x', 'grp_y'),...  39.2 us
    all_to_all x1, blocking collectives, per_device(): lax.all_to_all(power.reshape(16, 16, 128), ('grp_x', 'grp_y'), 0, 0, tile...  11.5 us
    pallas_call x1, Pallas kernels, project(): pl.pallas_call(project_kernel, out_shape=jax.ShapeDtypeStruct((512, 128),...  4.5 us

profile of v6, /device:TPU:1, one launch (start us, length us, event | category | flops | bytes accessed | tf_op | source)
XLA Modules:
  0.0 56.7 jit_solution(575832992178015339)
XLA Ops:
  0.0 0.0 copy-start
  0.0 0.0 copy-start.1
  0.0 0.0 copy-start.2
  0.0 0.0 copy-start.3
  0.0 4.5 %project.1 = f32[512,128]{1,0:T(8,128)S(1)} custom-call(s32[3,8]{1,0:T(4,128)} %q_hbm.1, s32[3,512]{1,0:T(4,128)} %cell_hbm.1, f32[1,240]{1,0:T(1,128)} %bitcast.10, bf16[16,240,512]{2,1,0:T(8,128)(2,1)} %vel_hbm.1, f32[2,8,240,240]{3,2,1,0:T(8,128)} %eig_hbm.1), custom_call_target="tpu_custom_call" | custom-call | tf_op jit(solution)/shard_map/project/pallas_call | solution.py:136
  4.5 39.2 %all_to_all.10 = f32[512,1,128]{2,1,0:T(1,128)S(1)} all-to-all(f32[512,1,128]{2,1,0:T(1,128)S(1)} %bitcast.7), channel_id=1, replica_groups=mesh['grp_y'=8,'grp_x'=2,'dev'=32] {'dev','grp_x','grp_y'}, dimensions={0} | all-to-all | bytes 524288 | tf_op jit(solution)/shard_map/all_to_all | solution.py:259
  43.8 0.0 copy-done
  43.8 0.0 copy-done.1
  43.8 0.0 copy-done.2
  43.8 0.0 copy-done.3
  43.8 0.7 %transform.1 = f32[256,128]{1,0:T(8,128)S(1)} custom-call(f32[512,128]{1,0:T(8,128)S(1)} %bitcast.8, bf16[2,128,128]{2,1,0:T(8,128)(2,1)S(1)} %copy-done.2, f32[8,16,128]{2,1,0:T(8,128)S(1)} %copy-done.1, bf16[2,128,256]{2,1,0:T(8,128)(2,1)S(1)} %copy-done, f32[8,128]{1,0:T(8,128)S(1)} %copy-done.3), custom_call_target="tpu_custom_call" | custom-call | tf_op jit(solution)/shard_map/transform/pallas_call | solution.py:247
  44.5 11.5 %all_to_all.11 = f32[16,16,128]{2,1,0:T(8,128)S(1)} all-to-all(f32[16,16,128]{2,1,0:T(8,128)S(1)} %bitcast.9), channel_id=1, replica_groups=mesh['grp_y'=8,'grp_x'=2,'dev'=32] {'grp_x','grp_y'}, dimensions={0} | all-to-all | bytes 262144 | tf_op jit(solution)/shard_map/all_to_all | solution.py:263
  56.0 0.7 %slice.5 = f32[15,16,128]{2,1,0:T(8,128)} slice(f32[16,16,128]{2,1,0:T(8,128)S(1)} %all_to_all.11), slice={[0:15], [0:16], [0:128]} | slice | bytes 245760 | tf_op jit(solution)/shard_map/slice | solution.py:266
Async XLA Ops:
  0.0 43.8 %copy-start = (bf16[2,128,256]{2,1,0:T(8,128)(2,1)S(1)}, bf16[2,128,256]{2,1,0:T(8,128)(2,1)}, u32[]{:S(2)}) copy-start(bf16[2,128,256]{2,1,0:T(8,128)(2,1)} %constant.10.clone.dft_ref) | copy-start | bytes 393220
  0.0 43.8 %copy-start.1 = (f32[8,16,128]{2,1,0:T(8,128)S(1)}, f32[8,16,128]{2,1,0:T(8,128)}, u32[]{:S(2)}) copy-start(f32[8,16,128]{2,1,0:T(8,128)} %constant.9.clone.twist_ref) | copy-start | bytes 196612
  0.0 43.8 %copy-start.2 = (bf16[2,128,128]{2,1,0:T(8,128)(2,1)S(1)}, bf16[2,128,128]{2,1,0:T(8,128)(2,1)}, u32[]{:S(2)}) copy-start(bf16[2,128,128]{2,1,0:T(8,128)(2,1)} %constant.8.clone.low_ref) | copy-start | bytes 196612
  0.0 43.8 %copy-start.3 = (f32[8,128]{1,0:T(8,128)S(1)}, f32[8,128]{1,0:T(8,128)}, u32[]{:S(2)}) copy-start(f32[8,128]{1,0:T(8,128)} %constant.11.clone.turn_ref) | copy-start | bytes 12292

commit v7 on v6

--- a/solution.py
+++ b/solution.py
@@ -21,7 +21,7 @@
 PER_DEV = 60
 QUAD = 4
 SPAN = 512
-GROUPS = np.arange(N_GRP).reshape(8, 2).T.ravel()
+GROUPS = np.arange(N_GRP).reshape(2, 4, 2).transpose(0, 2, 1).ravel()
 VEL_PARTS = 2
 EIG_PARTS = ((0, 4), (4, 8))
 EIG_STARTS = ((0,), (1,), ())
@@ -257,19 +257,19 @@
 def per_device(velocities, mass_root, eigvec, q_points, cell_offsets):
     messages = project(velocities, mass_root, eigvec, q_points, cell_offsets)
     frames = lax.all_to_all(
-        messages.reshape(512, 1, 128), ("dev", "grp_x", "grp_y"), 0, 0, tiled=True
+        messages.reshape(512, 1, 128), ("dev", "grp_high", "grp_x", "grp_low"), 0, 0, tiled=True
     )
     power = transform(frames.reshape(512, 128))
     spectra = lax.all_to_all(
-        power.reshape(16, 16, 128), ("grp_x", "grp_y"), 0, 0, tiled=True
+        power.reshape(16, 16, 128), ("grp_high", "grp_x", "grp_low"), 0, 0, tiled=True
     )
     rows = spectra.reshape(256, 128)[: PER_DEV * 4]
     return rows.reshape(1, PER_DEV, SPAN)
 
 
 def solution(mesh):
-    split_mesh = Mesh(mesh.devices.reshape(8, 2, N_DEV), ("grp_y", "grp_x", "dev"))
-    grp = ("grp_y", "grp_x")
+    grp = ("grp_high", "grp_low", "grp_x")
+    split_mesh = Mesh(mesh.devices.reshape(2, 4, 2, N_DEV), grp + ("dev",))
     return jax.shard_map(
         per_device,
         mesh=split_mesh,

time: 57.1 us -> 57.1 us (level)
  no operation moved by 1% of the time
where the time goes in v7:
time: 57.1 us; the launch traced here: 56.7 us
  blocking collectives  50.7 us (89%)
  Pallas kernels  5.22 us (9%)
  local copies, waits for them, and re-layouts  0.67 us (1%)
    all_to_all x1, blocking collectives, per_device(): lax.all_to_all(messages.reshape(512, 1, 128), ('dev', 'grp_high', 'grp_x'...  39.2 us
    all_to_all x1, blocking collectives, per_device(): lax.all_to_all(power.reshape(16, 16, 128), ('grp_high', 'grp_x', 'grp_low...  11.5 us
    pallas_call x1, Pallas kernels, project(): pl.pallas_call(project_kernel, out_shape=jax.ShapeDtypeStruct((512, 128),...  4.5 us

profile of v7, /device:TPU:1, one launch (start us, length us, event | category | flops | bytes accessed | tf_op | source)
XLA Modules:
  0.0 56.7 jit_solution(17537707373306154350)
XLA Ops:
  0.0 0.0 copy-start
  0.0 0.0 copy-start.1
  0.0 0.0 copy-start.2
  0.0 0.0 copy-start.3
  0.0 4.5 %project.1 = f32[512,128]{1,0:T(8,128)S(1)} custom-call(s32[3,8]{1,0:T(4,128)} %q_hbm.1, s32[3,512]{1,0:T(4,128)} %cell_hbm.1, f32[1,240]{1,0:T(1,128)} %bitcast.10, bf16[16,240,512]{2,1,0:T(8,128)(2,1)} %vel_hbm.1, f32[2,8,240,240]{3,2,1,0:T(8,128)} %eig_hbm.1), custom_call_target="tpu_custom_call" | custom-call | tf_op jit(solution)/shard_map/project/pallas_call | solution.py:136
  4.5 39.2 %all_to_all.10 = f32[512,1,128]{2,1,0:T(1,128)S(1)} all-to-all(f32[512,1,128]{2,1,0:T(1,128)S(1)} %bitcast.7), channel_id=1, replica_groups=mesh['grp_high'=2,'grp_low'=4,'grp_x'=2,'dev'=32] {'dev','grp_high','grp..., dimensions={0} | all-to-all | bytes 524288 | tf_op jit(solution)/shard_map/all_to_all | solution.py:259
  43.8 0.0 copy-done
  43.8 0.0 copy-done.1
  43.8 0.0 copy-done.2
  43.8 0.0 copy-done.3
  43.8 0.7 %transform.1 = f32[256,128]{1,0:T(8,128)S(1)} custom-call(f32[512,128]{1,0:T(8,128)S(1)} %bitcast.8, bf16[2,128,128]{2,1,0:T(8,128)(2,1)S(1)} %copy-done.2, f32[8,16,128]{2,1,0:T(8,128)S(1)} %copy-done.1, bf16[2,128,256]{2,1,0:T(8,128)(2,1)S(1)} %copy-done, f32[8,128]{1,0:T(8,128)S(1)} %copy-done.3), custom_call_target="tpu_custom_call" | custom-call | tf_op jit(solution)/shard_map/transform/pallas_call | solution.py:247
  44.5 11.5 %all_to_all.11 = f32[16,16,128]{2,1,0:T(8,128)S(1)} all-to-all(f32[16,16,128]{2,1,0:T(8,128)S(1)} %bitcast.9), channel_id=1, replica_groups=mesh['grp_high'=2,'grp_low'=4,'grp_x'=2,'dev'=32] {'grp_high','grp_x','g..., dimensions={0} | all-to-all | bytes 262144 | tf_op jit(solution)/shard_map/all_to_all | solution.py:263
  56.0 0.7 %slice.5 = f32[15,16,128]{2,1,0:T(8,128)} slice(f32[16,16,128]{2,1,0:T(8,128)S(1)} %all_to_all.11), slice={[0:15], [0:16], [0:128]} | slice | bytes 245760 | tf_op jit(solution)/shard_map/slice | solution.py:266
Async XLA Ops:
  0.0 43.8 %copy-start = (bf16[2,128,256]{2,1,0:T(8,128)(2,1)S(1)}, bf16[2,128,256]{2,1,0:T(8,128)(2,1)}, u32[]{:S(2)}) copy-start(bf16[2,128,256]{2,1,0:T(8,128)(2,1)} %constant.10.clone.dft_ref) | copy-start | bytes 393220
  0.0 43.8 %copy-start.1 = (f32[8,16,128]{2,1,0:T(8,128)S(1)}, f32[8,16,128]{2,1,0:T(8,128)}, u32[]{:S(2)}) copy-start(f32[8,16,128]{2,1,0:T(8,128)} %constant.9.clone.twist_ref) | copy-start | bytes 196612
  0.0 43.8 %copy-start.2 = (bf16[2,128,128]{2,1,0:T(8,128)(2,1)S(1)}, bf16[2,128,128]{2,1,0:T(8,128)(2,1)}, u32[]{:S(2)}) copy-start(bf16[2,128,128]{2,1,0:T(8,128)(2,1)} %constant.8.clone.low_ref) | copy-start | bytes 196612
  0.0 43.8 %copy-start.3 = (f32[8,128]{1,0:T(8,128)S(1)}, f32[8,128]{1,0:T(8,128)}, u32[]{:S(2)}) copy-start(f32[8,128]{1,0:T(8,128)} %constant.11.clone.turn_ref) | copy-start | bytes 12292

commit v8 on v7

--- a/solution.py
+++ b/solution.py
@@ -122,7 +122,7 @@
             imag_hi, imag_lo = split(eig[1, k])
             both = dot_t(jnp.concatenate([real_hi, real_lo], axis=0), first)
             both = both + dot_t(jnp.concatenate([imag_hi, imag_lo], axis=0), second)
-            series[k, :DOF, :] = (both[:DOF, :128] + both[:DOF, 128:]) + both[DOF:, :128]
+            series[k, :DOF, :] = both[:DOF, :128] + (both[:DOF, 128:] + both[DOF:, :128])
         for k in range(low, high):
             for chunk in range(4):
                 message = None

time: 57.1 us -> 57.1 us (level)
  no operation moved by 1% of the time
where the time goes in v8:
time: 57.1 us; the launch traced here: 56.7 us
  blocking collectives  50.7 us (89%)
  Pallas kernels  5.2 us (9%)
  local copies, waits for them, and re-layouts  0.67 us (1%)
    all_to_all x1, blocking collectives, per_device(): lax.all_to_all(messages.reshape(512, 1, 128), ('dev', 'grp_high', 'grp_x'...  39.2 us
    all_to_all x1, blocking collectives, per_device(): lax.all_to_all(power.reshape(16, 16, 128), ('grp_high', 'grp_x', 'grp_low...  11.5 us
    pallas_call x1, Pallas kernels, project(): pl.pallas_call(project_kernel, out_shape=jax.ShapeDtypeStruct((512, 128),...  4.49 us

profile of v8, /device:TPU:1, one launch (start us, length us, event | category | flops | bytes accessed | tf_op | source)
XLA Modules:
  0.0 56.7 jit_solution(10455555393349446942)
XLA Ops:
  0.0 0.0 copy-start
  0.0 0.0 copy-start.1
  0.0 0.0 copy-start.2
  0.0 0.0 copy-start.3
  0.0 4.5 %project.1 = f32[512,128]{1,0:T(8,128)S(1)} custom-call(s32[3,8]{1,0:T(4,128)} %q_hbm.1, s32[3,512]{1,0:T(4,128)} %cell_hbm.1, f32[1,240]{1,0:T(1,128)} %bitcast.10, bf16[16,240,512]{2,1,0:T(8,128)(2,1)} %vel_hbm.1, f32[2,8,240,240]{3,2,1,0:T(8,128)} %eig_hbm.1), custom_call_target="tpu_custom_call" | custom-call | tf_op jit(solution)/shard_map/project/pallas_call | solution.py:136
  4.5 39.2 %all_to_all.10 = f32[512,1,128]{2,1,0:T(1,128)S(1)} all-to-all(f32[512,1,128]{2,1,0:T(1,128)S(1)} %bitcast.7), channel_id=1, replica_groups=mesh['grp_high'=2,'grp_low'=4,'grp_x'=2,'dev'=32] {'dev','grp_high','grp..., dimensions={0} | all-to-all | bytes 524288 | tf_op jit(solution)/shard_map/all_to_all | solution.py:259
  43.7 0.0 copy-done
  43.8 0.0 copy-done.1
  43.8 0.0 copy-done.2
  43.8 0.0 copy-done.3
  43.8 0.7 %transform.1 = f32[256,128]{1,0:T(8,128)S(1)} custom-call(f32[512,128]{1,0:T(8,128)S(1)} %bitcast.8, bf16[2,128,128]{2,1,0:T(8,128)(2,1)S(1)} %copy-done.2, f32[8,16,128]{2,1,0:T(8,128)S(1)} %copy-done.1, bf16[2,128,256]{2,1,0:T(8,128)(2,1)S(1)} %copy-done, f32[8,128]{1,0:T(8,128)S(1)} %copy-done.3), custom_call_target="tpu_custom_call" | custom-call | tf_op jit(solution)/shard_map/transform/pallas_call | solution.py:247
  44.5 11.5 %all_to_all.11 = f32[16,16,128]{2,1,0:T(8,128)S(1)} all-to-all(f32[16,16,128]{2,1,0:T(8,128)S(1)} %bitcast.9), channel_id=1, replica_groups=mesh['grp_high'=2,'grp_low'=4,'grp_x'=2,'dev'=32] {'grp_high','grp_x','g..., dimensions={0} | all-to-all | bytes 262144 | tf_op jit(solution)/shard_map/all_to_all | solution.py:263
  56.0 0.7 %slice.5 = f32[15,16,128]{2,1,0:T(8,128)} slice(f32[16,16,128]{2,1,0:T(8,128)S(1)} %all_to_all.11), slice={[0:15], [0:16], [0:128]} | slice | bytes 245760 | tf_op jit(solution)/shard_map/slice | solution.py:266
Async XLA Ops:
  0.0 43.8 %copy-start = (bf16[2,128,256]{2,1,0:T(8,128)(2,1)S(1)}, bf16[2,128,256]{2,1,0:T(8,128)(2,1)}, u32[]{:S(2)}) copy-start(bf16[2,128,256]{2,1,0:T(8,128)(2,1)} %constant.10.clone.dft_ref) | copy-start | bytes 393220
  0.0 43.8 %copy-start.1 = (f32[8,16,128]{2,1,0:T(8,128)S(1)}, f32[8,16,128]{2,1,0:T(8,128)}, u32[]{:S(2)}) copy-start(f32[8,16,128]{2,1,0:T(8,128)} %constant.9.clone.twist_ref) | copy-start | bytes 196612
  0.0 43.8 %copy-start.2 = (bf16[2,128,128]{2,1,0:T(8,128)(2,1)S(1)}, bf16[2,128,128]{2,1,0:T(8,128)(2,1)}, u32[]{:S(2)}) copy-start(bf16[2,128,128]{2,1,0:T(8,128)(2,1)} %constant.8.clone.low_ref) | copy-start | bytes 196612
  0.0 43.8 %copy-start.3 = (f32[8,128]{1,0:T(8,128)S(1)}, f32[8,128]{1,0:T(8,128)}, u32[]{:S(2)}) copy-start(f32[8,128]{1,0:T(8,128)} %constant.11.clone.turn_ref) | copy-start | bytes 12292
